TPU v7x, 512 devices: a whole 4x8x8 slice. The times are simulated.
512 devices in a mesh: freq: 16 (over z_lo, x), layer: 32 (over z_hi, y, core).
Axes of the slice: x: 4, y: 8, z: 8 (z_hi: 2, z_lo: 4; z = z_hi * 4 + z_lo), core: 2. Of those that a mesh axis runs over, the one named last changes fastest.
Arguments:
- conductivity: float32 [32, 128, 128], P('layer'), may hold values from 0.1 to 1
- background: float32 [16, 2, 2, 32, 128, 128], P('freq', None, None, 'layer'), may hold values from -6 to 6
- green: float32 [16, 2, 32, 256, 256], P('freq', None, None, 'layer'), may hold values from -2 to 2
- pair_table: int32 [32, 32], replicated, may hold values from 0 to 31, as said below
- stations: int32 [32, 128], P('layer'), may hold values from 0 to 16383, as said below
- observed: float32 [16, 2, 2, 32, 128], P('freq', None, None, 'layer'), may hold values from -6 to 6
- data_error: float32 [16, 2, 32, 128], P('freq', None, 'layer'), may hold values from 0.3 to 3
Outputs:
- gradient: float32 [32, 128, 128], P('layer')
Inputs may be any that keep to these rules, and one draw needn't show every extreme that they name: pair_table[i, j] == pair_table[j, i]. row-major cell index x * 128 + y within the station's layer; stations may share a cell.
All inputs are finite; a program needn't handle non-finite values.
Results may differ from a plain program's by a relative error of at most 0.000073.
Values sent between devices are 32-bit elements; how exact they have to be, the bound alone decides.
No kernel may reach another device: no remote copies, remote signals or barrier semaphores. Data moves between devices by JAX's collectives and lax.ppermute only.
A program may use at most 64 MiB of HBM per device.

v0:
```python
import math

import jax
import jax.numpy as jnp
from jax import lax
from jax.sharding import PartitionSpec as P

HIGHEST = lax.Precision.HIGHEST


def dft_tables(wave_count, cell_count):
    wave_ids = jnp.arange(wave_count, dtype=jnp.int32)[:, None]
    cell_ids = jnp.arange(cell_count, dtype=jnp.int32)[None, :]
    phases = wave_ids * cell_ids % wave_count
    angles = phases.astype(jnp.float32) * (2.0 * math.pi / wave_count)
    return (jnp.cos(angles), jnp.sin(angles))


def forward_rows(re_part, im_part, cosine_table, sine_table):
    cos_re = jnp.einsum("kx,...xy->...ky", cosine_table, re_part, precision=HIGHEST)
    cos_im = jnp.einsum("kx,...xy->...ky", cosine_table, im_part, precision=HIGHEST)
    sin_re = jnp.einsum("kx,...xy->...ky", sine_table, re_part, precision=HIGHEST)
    sin_im = jnp.einsum("kx,...xy->...ky", sine_table, im_part, precision=HIGHEST)
    return (cos_re + sin_im, cos_im - sin_re)


def forward_cols(re_part, im_part, cosine_table, sine_table):
    cos_re = jnp.einsum("...y,ky->...k", re_part, cosine_table, precision=HIGHEST)
    cos_im = jnp.einsum("...y,ky->...k", im_part, cosine_table, precision=HIGHEST)
    sin_re = jnp.einsum("...y,ky->...k", re_part, sine_table, precision=HIGHEST)
    sin_im = jnp.einsum("...y,ky->...k", im_part, sine_table, precision=HIGHEST)
    return (cos_re + sin_im, cos_im - sin_re)


def inverse_cols(re_part, im_part, cosine_table, sine_table):
    scale = 1.0 / cosine_table.shape[0]
    cos_re = jnp.einsum("...k,ky->...y", re_part, cosine_table, precision=HIGHEST)
    cos_im = jnp.einsum("...k,ky->...y", im_part, cosine_table, precision=HIGHEST)
    sin_re = jnp.einsum("...k,ky->...y", re_part, sine_table, precision=HIGHEST)
    sin_im = jnp.einsum("...k,ky->...y", im_part, sine_table, precision=HIGHEST)
    return ((cos_re - sin_im) * scale, (cos_im + sin_re) * scale)


def inverse_rows(re_part, im_part, cosine_table, sine_table):
    scale = 1.0 / cosine_table.shape[0]
    cos_re = jnp.einsum("kx,...ky->...xy", cosine_table, re_part, precision=HIGHEST)
    cos_im = jnp.einsum("kx,...ky->...xy", cosine_table, im_part, precision=HIGHEST)
    sin_re = jnp.einsum("kx,...ky->...xy", sine_table, re_part, precision=HIGHEST)
    sin_im = jnp.einsum("kx,...ky->...xy", sine_table, im_part, precision=HIGHEST)
    return ((cos_re - sin_im) * scale, (cos_im + sin_re) * scale)


def mix_layers(spec_real, spec_imag, green_real, green_imag, pair_table):

    def one_receiver(table_row):
        row_real = jnp.take(green_real, table_row, axis=0)
        row_imag = jnp.take(green_imag, table_row, axis=0)
        out_real = jnp.sum(row_real * spec_real - row_imag * spec_imag, axis=1)
        out_imag = jnp.sum(row_real * spec_imag + row_imag * spec_real, axis=1)
        return (out_real, out_imag)

    mixed_real, mixed_imag = lax.map(one_receiver, pair_table)
    return (jnp.moveaxis(mixed_real, 0, 1), jnp.moveaxis(mixed_imag, 0, 1))


def apply_green(src_real, src_imag, green_real, green_imag, pair_table):
    x_cells = src_real.shape[-2]
    y_cells = src_real.shape[-1]
    cosine_x, sine_x = dft_tables(2 * x_cells, x_cells)
    cosine_y, sine_y = dft_tables(2 * y_cells, y_cells)
    rows_real, rows_imag = forward_rows(src_real, src_imag, cosine_x, sine_x)
    spec_real, spec_imag = forward_cols(rows_real, rows_imag, cosine_y, sine_y)
    mixed = mix_layers(
        lax.all_to_all(spec_real, "layer", split_axis=2, concat_axis=1, tiled=True),
        lax.all_to_all(spec_imag, "layer", split_axis=2, concat_axis=1, tiled=True),
        green_real,
        green_imag,
        pair_table,
    )
    back_real, back_imag = (
        lax.all_to_all(mixed[0], "layer", split_axis=1, concat_axis=2, tiled=True),
        lax.all_to_all(mixed[1], "layer", split_axis=1, concat_axis=2, tiled=True),
    )
    cols_real, cols_imag = inverse_cols(back_real, back_imag, cosine_y, sine_y)
    return inverse_rows(cols_real, cols_imag, cosine_x, sine_x)


def station_values(total_real, total_imag, stations, measured, errors):
    pol_count = total_real.shape[0]
    layer_count = total_real.shape[1]
    flat_real = total_real.reshape(pol_count, layer_count, -1)
    flat_imag = total_imag.reshape(pol_count, layer_count, -1)
    station_idx = jnp.broadcast_to(stations[None], (pol_count,) + stations.shape)
    pred_real = jnp.take_along_axis(flat_real, station_idx, axis=2)
    pred_imag = jnp.take_along_axis(flat_imag, station_idx, axis=2)
    weight = errors * errors
    return ((pred_real - measured[:, 0]) / weight, (pred_imag - measured[:, 1]) / weight)


def scatter_source(resid_real, resid_imag, stations, field_shape):
    pol_count, layer_count = (field_shape[0], field_shape[1])
    cells = field_shape[2] * field_shape[3]
    layer_ids = jnp.arange(layer_count, dtype=jnp.int32)[:, None]
    source_real = (
        jnp.zeros((pol_count, layer_count, cells), jnp.float32)
        .at[:, layer_ids, stations]
        .add(resid_real)
    )
    source_imag = (
        jnp.zeros((pol_count, layer_count, cells), jnp.float32)
        .at[:, layer_ids, stations]
        .add(-resid_imag)
    )
    return (source_real.reshape(field_shape), source_imag.reshape(field_shape))


def per_device(conductivity, background, green, pair_table, stations, observed, data_error):
    field_pair = background[0]
    bg_real = field_pair[:, 0]
    bg_imag = field_pair[:, 1]
    green_real = green[0, 0]
    green_imag = green[0, 1]
    scat_real, scat_imag = apply_green(
        conductivity * bg_real, conductivity * bg_imag, green_real, green_imag, pair_table
    )
    total_real = bg_real + scat_real
    total_imag = bg_imag + scat_imag
    resid_real, resid_imag = station_values(
        total_real, total_imag, stations, observed[0], data_error[0]
    )
    source_real, source_imag = scatter_source(resid_real, resid_imag, stations, total_real.shape)
    adj_real, adj_imag = apply_green(source_real, source_imag, green_real, green_imag, pair_table)
    local_term = jnp.sum(total_real * adj_real - total_imag * adj_imag, axis=0)
    return lax.psum(local_term, "freq")


def solution(mesh):
    in_specs = (
        P("layer", None, None),
        P("freq", None, None, "layer", None, None),
        P("freq", None, None, "layer", None),
        P(),
        P("layer", None),
        P("freq", None, None, "layer", None),
        P("freq", None, "layer", None),
    )
    out_specs = P("layer", None, None)
    return jax.shard_map(
        per_device, mesh=mesh, in_specs=in_specs, out_specs=out_specs, check_vma=False
    )
```

profile of v0, /device:TPU:8, one launch (start us, length us, event | category | flops | bytes accessed | tf_op | source)
XLA Modules:
  0.0 622.1 jit_solution(12864283717387447946)
XLA Ops:
  6.5 1.1 copy.68
  11.2 1.1 fusion.95
  13.2 1.1 fusion.9
  14.3 1.2 copy.72
  15.4 16.1 %all-to-all-start = ((f32[2,1,256,256]{3,0,1,2:T(2,128)}), f32[2,1,256,256]{3,0,1,2:T(2,128)S(1)}, u32[]{:S(2)}, u32[]{:S(2)}) async-start(f32[2,1,256,256]{3,0,1,2:T(2,128)} %copy.72), calls=%async_computation | async-start | bytes 1048576 | tf_op jit(solution)/shard_map/all_to_all | solution.py:74
  31.6 1.1 fusion.91
  32.7 1.1 fusion.8
  33.7 1.2 copy.75
  35.0 18.5 %all-to-all-done = f32[2,1,256,256]{3,0,1,2:T(2,128)S(1)} async-done(((f32[2,1,256,256]{3,0,1,2:T(2,128)}), f32[2,1,256,256]{3,0,1,2:T(2,128)S(1)}, u32[]{:S(2)}, u32[]{:S(2)}) %all-to-all-start) | async-done | bytes 524320 | tf_op jit(solution)/shard_map/all_to_all | solution.py:74
  53.4 4.3 all-to-all-start.1
  57.8 21.8 %all-to-all-done.1 = f32[2,1,256,256]{3,0,1,2:T(2,128)S(1)} async-done(((f32[2,1,256,256]{3,0,1,2:T(2,128)}), f32[2,1,256,256]{3,0,1,2:T(2,128)S(1)}, u32[]{:S(2)}, u32[]{:S(2)}) %all-to-all-start.1) | async-done | bytes 524320 | tf_op jit(solution)/shard_map/all_to_all | solution.py:75
  81.4 88.7 %while.24 = (s32[]{:T(128)}, f32[32,2,8,256]{3,2,1,0:T(8,128)}, f32[32,2,8,256]{3,2,1,0:T(8,128)}, s32[32,32]{1,0:T(8,128)}, f32[32,8,256]{2,1,0:T(8,128)S(1)}, ...) while((s32[]{:T(128)}, f32[32,2,8,256]{3,2,1,0:T(8,128)}, ...), condition=%wide.region_3.5_spmd, body=%wide.region_0.4_spmd.sunk | while | flops 1172674 | bytes 3773729 | solution.py:62
  170.2 4.3 all-to-all-start.2
  174.6 21.9 %all-to-all-done.2 = f32[2,32,8,256]{3,2,0,1:T(8,128)S(1)} async-done(((f32[2,32,8,256]{3,2,0,1:T(8,128)}), f32[2,32,8,256]{3,2,0,1:T(8,128)S(1)}, u32[]{:S(2)}, u32[]{:S(2)}) %all-to-all-start.2) | async-done | bytes 524320 | tf_op jit(solution)/shard_map/all_to_all | solution.py:81
  196.4 4.6 all-to-all-start.3
  201.1 1.1 fusion.42
  202.2 20.7 %all-to-all-done.3 = f32[2,32,8,256]{3,2,0,1:T(8,128)S(1)} async-done(((f32[2,32,8,256]{3,2,0,1:T(8,128)}), f32[2,32,8,256]{3,2,0,1:T(8,128)S(1)}, u32[]{:S(2)}, u32[]{:S(2)}) %all-to-all-start.3) | async-done | bytes 524320 | tf_op jit(solution)/shard_map/all_to_all | solution.py:82
  222.8 1.1 fusion.14
  224.9 1.1 fusion.38
  225.9 1.1 fusion.15
  228.0 1.0 fusion.26
  230.4 2.5 gather_fusion.4
  232.9 2.5 gather_fusion.5
  235.5 4.9 scatter_custom_fusion.1
  240.4 6.6 %copy.90 = f32[2,128,128]{1,2,0:T(8,128)S(1)} copy(f32[2,128,128]{0,2,1:T(8,128)} %bitcast.285) | data formatting | bytes 262144 | tf_op jit(solution)/shard_map/reshape.56
  248.0 4.7 scatter_custom_fusion
  252.7 6.6 %copy.85 = f32[2,128,128]{1,2,0:T(8,128)S(1)} copy(f32[2,128,128]{0,2,1:T(8,128)} %bitcast.284) | data formatting | bytes 262144 | tf_op jit(solution)/shard_map/reshape.49
  261.0 1.1 fusion.77
  262.9 1.1 fusion.6
  264.0 1.2 copy.98
  265.2 4.7 all-to-all-start.5
  269.9 1.1 fusion.81
  271.0 1.1 fusion.7
  272.1 1.2 copy.95
  273.3 18.5 %all-to-all-done.5 = f32[2,1,256,256]{3,0,1,2:T(2,128)S(1)} async-done(((f32[2,1,256,256]{3,0,1,2:T(2,128)}), f32[2,1,256,256]{3,0,1,2:T(2,128)S(1)}, u32[]{:S(2)}, u32[]{:S(2)}) %all-to-all-start.5) | async-done | bytes 524320 | tf_op jit(solution)/shard_map/all_to_all | solution.py:75
  291.7 4.4 all-to-all-start.4
  296.1 21.9 %all-to-all-done.4 = f32[2,1,256,256]{3,0,1,2:T(2,128)S(1)} async-done(((f32[2,1,256,256]{3,0,1,2:T(2,128)}), f32[2,1,256,256]{3,0,1,2:T(2,128)S(1)}, u32[]{:S(2)}, u32[]{:S(2)}) %all-to-all-start.4) | async-done | bytes 524320 | tf_op jit(solution)/shard_map/all_to_all | solution.py:74
  319.0 88.3 %while.25 = (s32[]{:T(128)}, f32[32,2,8,256]{3,2,1,0:T(8,128)}, f32[32,2,8,256]{3,2,1,0:T(8,128)S(1)}, s32[32,32]{1,0:T(8,128)}, f32[32,8,256]{2,1,0:T(8,128)S(1...) while((s32[]{:T(128)}, f32[32,2,8,256]{3,2,1,0:T(8,128)}, ...), condition=%wide.region_9.12_spmd, body=%wide.region_6.11_spmd.sunk | while | flops 1172674 | bytes 3773729 | solution.py:62
  407.3 25.3 %all_to_all.84 = f32[2,32,8,256]{3,2,0,1:T(8,128)S(1)} all-to-all(f32[2,32,8,256]{3,2,0,1:T(8,128)S(1)} %bitcast.292), channel_id=1, replica_groups=mesh['freq'=16,'layer'=32] {'layer'}, dimensions={1} | all-to-all | bytes 1048576 | tf_op jit(solution)/shard_map/all_to_all | solution.py:82
  432.7 4.3 all-to-all-start.6
  437.0 1.1 fusion.32
  438.1 20.8 %all-to-all-done.6 = f32[2,32,8,256]{3,2,0,1:T(8,128)S(1)} async-done(((f32[2,32,8,256]{3,2,0,1:T(8,128)}), f32[2,32,8,256]{3,2,0,1:T(8,128)S(1)}, u32[]{:S(2)}, u32[]{:S(2)}) %all-to-all-start.6) | async-done | bytes 524320 | tf_op jit(solution)/shard_map/all_to_all | solution.py:81
  458.9 1.1 fusion.17
  461.0 1.1 fusion.36
  462.0 1.1 fusion.16
  465.0 1.6 fusion.31
  466.7 146.6 %all-reduce.3.cloned.1.call-done = f32[1,128,128]{1,2,0:T(8,128)} async-done(((f32[1,128,128]{1,2,0:T(8,128)}), f32[1,128,128]{1,2,0:T(8,128)}) %all-reduce.3.cloned.1.call-update) | async-done | bytes 65552 | tf_op jit(solution)/shard_map/psum | solution.py:134
  613.3 1.6 copy.107
  (497 shorter events, 191.9 us)
Async XLA Ops:
  6.5 51.2 %copy-start = (f32[1,2,32,8,256]{4,3,2,1,0:T(8,128)S(1)}, f32[1,2,32,8,256]{4,3,2,1,0:T(8,128)}, u32[]{:S(2)}) copy-start(f32[1,2,32,8,256]{4,3,2,1,0:T(8,128)} %param.17) | copy-start | bytes 1572868
  15.4 38.0 %all-to-all-start = ((f32[2,1,256,256]{3,0,1,2:T(2,128)}), f32[2,1,256,256]{3,0,1,2:T(2,128)S(1)}, u32[]{:S(2)}, u32[]{:S(2)}) async-start(f32[2,1,256,256]{3,0,1,2:T(2,128)} %copy.72), calls=%async_computation | async-start | bytes 1048576 | tf_op jit(solution)/shard_map/all_to_all | solution.py:74
  53.4 26.2 %all-to-all-start.1 = ((f32[2,1,256,256]{3,0,1,2:T(2,128)}), f32[2,1,256,256]{3,0,1,2:T(2,128)S(1)}, u32[]{:S(2)}, u32[]{:S(2)}) async-start(f32[2,1,256,256]{3,0,1,2:T(2,128)} %copy.75), calls=%async_computation.1 | async-start | bytes 1048576 | tf_op jit(solution)/shard_map/all_to_all | solution.py:75
  81.4 93.1 %copy-start.3 = (f32[1,2,2,1,128]{4,3,2,1,0:T(1,128)S(1)}, f32[1,2,2,1,128]{4,3,2,1,0:T(1,128)}, u32[]{:S(2)}) copy-start(f32[1,2,2,1,128]{4,3,2,1,0:T(1,128)} %param.20) | copy-start | bytes 6148
  81.4 93.1 %copy-start.1 = (f32[1,2,1,128]{3,2,1,0:T(1,128)S(1)}, f32[1,2,1,128]{3,2,1,0:T(1,128)}, u32[]{:S(2)}) copy-start(f32[1,2,1,128]{3,2,1,0:T(1,128)} %param.21) | copy-start | bytes 3076
  81.4 93.1 %copy-start.2 = (s32[1,128]{1,0:T(1,128)S(1)}, s32[1,128]{1,0:T(1,128)}, u32[]{:S(2)}) copy-start(s32[1,128]{1,0:T(1,128)} %param.19) | copy-start | bytes 1540
  170.2 26.3 %all-to-all-start.2 = ((f32[2,32,8,256]{3,2,0,1:T(8,128)}), f32[2,32,8,256]{3,2,0,1:T(8,128)S(1)}, u32[]{:S(2)}, u32[]{:S(2)}) async-start(f32[2,32,8,256]{3,2,0,1:T(8,128)} %bitcast.29), calls=%async_computation.2 | async-start | bytes 1048576 | tf_op jit(solution)/shard_map/all_to_all | solution.py:81
  196.4 26.4 %all-to-all-start.3 = ((f32[2,32,8,256]{3,2,0,1:T(8,128)}), f32[2,32,8,256]{3,2,0,1:T(8,128)S(1)}, u32[]{:S(2)}, u32[]{:S(2)}) async-start(f32[2,32,8,256]{3,2,0,1:T(8,128)} %bitcast.31), calls=%async_computation.3 | async-start | bytes 1048576 | tf_op jit(solution)/shard_map/all_to_all | solution.py:82
  265.2 26.5 %all-to-all-start.5 = ((f32[2,1,256,256]{3,0,1,2:T(2,128)}), f32[2,1,256,256]{3,0,1,2:T(2,128)S(1)}, u32[]{:S(2)}, u32[]{:S(2)}) async-start(f32[2,1,256,256]{3,0,1,2:T(2,128)} %copy.98), calls=%async_computation.5 | async-start | bytes 1048576 | tf_op jit(solution)/shard_map/all_to_all | solution.py:75
  291.7 26.3 %all-to-all-start.4 = ((f32[2,1,256,256]{3,0,1,2:T(2,128)}), f32[2,1,256,256]{3,0,1,2:T(2,128)S(1)}, u32[]{:S(2)}, u32[]{:S(2)}) async-start(f32[2,1,256,256]{3,0,1,2:T(2,128)} %copy.95), calls=%async_computation.4 | async-start | bytes 1048576 | tf_op jit(solution)/shard_map/all_to_all | solution.py:74
  432.7 26.3 %all-to-all-start.6 = ((f32[2,32,8,256]{3,2,0,1:T(8,128)}), f32[2,32,8,256]{3,2,0,1:T(8,128)S(1)}, u32[]{:S(2)}, u32[]{:S(2)}) async-start(f32[2,32,8,256]{3,2,0,1:T(8,128)} %bitcast.74), calls=%async_computation.6 | async-start | bytes 1048576 | tf_op jit(solution)/shard_map/all_to_all | solution.py:81
  437.0 176.3 %all-reduce.3.cloned.1.call-start = ((), (), s32[]{:S(2)}) async-start(), calls=%async_computation.8 | async-start | bytes 131072 | tf_op jit(solution)/shard_map/psum | solution.py:134
Sparse Core Ops, SparseCore 0:
  466.8 146.4 all-reduce.2
where the time goes:
time: 633 us; the launch traced here: 622 us
  waiting for transfers between devices  291 us (46%)
  local copies, waits for them, and re-layouts  144 us (23%)
  other arithmetic  70.3 us (11%)
  starting transfers between devices  42.8 us (7%)
  matrix products  32.3 us (5%)
  blocking collectives  25.3 us (4%)
  between operations  14.3 us (2%)
    psum x1, waiting for transfers between devices, per_device(): return lax.psum(local_term, 'freq')  147 us
    and x64, other arithmetic, one_receiver(): row_real = jnp.take(green_real, table_row, axis=0)  44.6 us
    all_to_all x2, waiting for transfers between devices, apply_green(): lax.all_to_all(mixed[0], 'layer', split_axis=1, concat_axis=2, tiled=True)  42.7 us
    all_to_all x2, waiting for transfers between devices, apply_green(): lax.all_to_all(spec_real, 'layer', split_axis=2, concat_axis=1, tiled=True)  40.4 us
    all_to_all x2, waiting for transfers between devices, apply_green(): lax.all_to_all(spec_imag, 'layer', split_axis=2, concat_axis=1, tiled=True)  40.3 us
    dynamic_update_slice x64, local copies, waits for them, and re-layouts, mix_layers(): mixed_real, mixed_imag = lax.map(one_receiver, pair_table)  39.3 us
    gather x64, local copies, waits for them, and re-layouts, one_receiver(): row_real = jnp.take(green_real, table_row, axis=0)  37.5 us
    gather x64, local copies, waits for them, and re-layouts, one_receiver(): row_imag = jnp.take(green_imag, table_row, axis=0)  37.5 us
  transfers between devices with their start and end apart: 8, of which 8 were waited for; matrix products, arithmetic and copies ran while one was open for 1% of the time, Pallas kernels for 0%

commit v1 on v0

v1 whole, which is shorter than its diff:
```python
import functools
import math

import jax
import jax.numpy as jnp
import ml_dtypes
import numpy as np
from jax import lax
from jax.experimental import pallas as pl
from jax.experimental.pallas import tpu as pltpu
from jax.sharding import PartitionSpec as P

CELLS = 128
WAVES = 256
LAYERS = 32
ROWS = 8
POLS = 2
GROUP = 4
STEP = 8
RING = 4
F32 = jnp.float32
BF16 = jnp.bfloat16
VMEM_BYTES = 40 * 1024 * 1024


def halves(table):
    high = table.astype(ml_dtypes.bfloat16)
    low = (table - high.astype(np.float64)).astype(ml_dtypes.bfloat16)
    return high, low


def dft_blocks():
    waves = np.arange(WAVES)[:, None]
    cells = np.arange(CELLS)[None, :]
    angles = (waves * cells % WAVES) * (2.0 * math.pi / WAVES)
    cos, sin = np.cos(angles), np.sin(angles)
    x_fwd = np.block([[cos, sin], [-sin, cos]])
    y_fwd = np.block([[cos.T, -sin.T], [sin.T, cos.T]])
    y_inv = np.block([[cos, sin], [-sin, cos]]) / WAVES
    x_inv = np.block([[cos.T, -sin.T], [sin.T, cos.T]]) / WAVES
    return x_fwd, y_fwd, y_inv, x_inv


def left_table(table):
    high, low = halves(table)
    return np.concatenate([high, high, low], axis=1)


def right_table(table):
    high, low = halves(table)
    return np.concatenate([high, high, low], axis=0)


def split_cat(values, axis):
    high = values.astype(BF16)
    low = (values - high.astype(F32)).astype(BF16)
    return jnp.concatenate([high, low, high], axis=axis)


def x_forward_kernel(cond_ref, field_ref, table_ref, out_ref):
    cond = cond_ref[0]
    parts = [
        jnp.concatenate([cond * field_ref[0, p, c, 0] for p in range(POLS)], axis=1)
        for c in range(2)
    ]
    cells = jnp.concatenate(parts, axis=0)
    rows = jnp.dot(table_ref[...], split_cat(cells, 0), preferred_element_type=F32)
    for p in range(POLS):
        for c in range(2):
            block = rows[c * WAVES : (c + 1) * WAVES, p * CELLS : (p + 1) * CELLS]
            out_ref[:, 2 * p + c] = block.reshape(LAYERS, ROWS, CELLS)


def mix_rows(rows_ref, green_ref, pair_ref, fwd_ref, inv_ref, out_ref, spec_ref, kern_ref, mixed_ref):
    for h in range(2):
        lanes = slice(h * CELLS, (h + 1) * CELLS)
        g_re = green_ref[0, 0, :, :, lanes]
        g_im = green_ref[0, 1, :, :, lanes]
        kern_ref[h, :, 0] = g_re + g_im
        kern_ref[h, :, 1] = g_re
        kern_ref[h, :, 2] = g_im
    for p in range(POLS):
        flat = [rows_ref[:, 2 * p + c].reshape(LAYERS * ROWS, CELLS) for c in range(2)]
        both = jnp.concatenate(flat, axis=1)
        spec = jnp.dot(split_cat(both, 1), fwd_ref[...], preferred_element_type=F32)
        for h in range(2):
            re = spec[:, h * CELLS : (h + 1) * CELLS].reshape(LAYERS, ROWS, CELLS)
            im = spec[:, WAVES + h * CELLS : WAVES + (h + 1) * CELLS].reshape(LAYERS, ROWS, CELLS)
            spec_ref[h, :, 3 * p] = re
            spec_ref[h, :, 3 * p + 1] = im - re
            spec_ref[h, :, 3 * p + 2] = re + im

    for h in range(2):

        def one_group(group, carry, h=h):
            first = group * GROUP

            def some_sources(chunk, sums):
                sums = list(sums)
                for s in range(STEP):
                    j = chunk * STEP + s
                    src = [spec_ref[h, j, k] for k in range(3 * POLS)]
                    for r in range(GROUP):
                        n = pair_ref[first + r, j]
                        kern = [kern_ref[h, n, k] for k in range(3)]
                        for p in range(POLS):
                            for k in range(3):
                                at = (r * POLS + p) * 3 + k
                                sums[at] = sums[at] + kern[k] * src[3 * p + k]
                return tuple(sums)

            zero = jnp.zeros((ROWS, CELLS), F32)
            sums = lax.fori_loop(
                0, LAYERS // STEP, some_sources, (zero,) * (GROUP * POLS * 3)
            )
            for r in range(GROUP):
                for p in range(POLS):
                    one, two, three = sums[(r * POLS + p) * 3 : (r * POLS + p) * 3 + 3]
                    mixed_ref[p, first + r, :, h * CELLS : (h + 1) * CELLS] = one - three
                    mixed_ref[p, first + r, :, WAVES + h * CELLS : WAVES + (h + 1) * CELLS] = one + two
            return carry

        lax.fori_loop(0, LAYERS // GROUP, one_group, 0)

    for p in range(POLS):
        mixed = mixed_ref[p].reshape(LAYERS * ROWS, 2 * WAVES)
        back = jnp.dot(split_cat(mixed, 1), inv_ref[...], preferred_element_type=F32)
        for c in range(2):
            out_ref[:, 2 * p + c] = back[:, c * CELLS : (c + 1) * CELLS].reshape(LAYERS, ROWS, CELLS)


def mix_kernel(pair_ref, rows_ref, green_ref, fwd_ref, inv_ref, out_ref, spec_ref, kern_ref, mixed_ref):
    mix_rows(rows_ref, green_ref, pair_ref, fwd_ref, inv_ref, out_ref, spec_ref, kern_ref, mixed_ref)


def sin_pi(v):
    square = v * v
    total = jnp.full_like(v, math.pi**13 / math.factorial(13))
    for order in (11, 9, 7, 5, 3, 1):
        sign = -1.0 if (order // 2) % 2 else 1.0
        total = total * square + sign * math.pi**order / math.factorial(order)
    return total * v


def adjoint_mix_kernel(
    pair_ref, first_ref, sent_ref, green_ref, fwd_ref, inv_ref,
    out_ref, rows_ref, spec_ref, kern_ref, mixed_ref,
):
    cell = sent_ref[:, 4:5, :].astype(jnp.int32)
    x_cell = cell >> 7
    wave = first_ref[0] + lax.broadcasted_iota(jnp.int32, (LAYERS, ROWS, CELLS), 1)
    turn = (wave * x_cell) & (WAVES - 1)
    u = (turn.astype(F32) - WAVES / 2) * (2.0 / WAVES)
    size = jnp.abs(u)
    cos = -sin_pi(0.5 - size)
    sin = sin_pi(jnp.minimum(size, 1.0 - size))
    sin = jnp.where(u < 0, sin, -sin)
    for p in range(POLS):
        re = sent_ref[:, 2 * p : 2 * p + 1, :]
        im = sent_ref[:, 2 * p + 1 : 2 * p + 2, :]
        rows_ref[:, 2 * p] = re * cos + im * sin
        rows_ref[:, 2 * p + 1] = im * cos - re * sin
    y_ids = lax.broadcasted_iota(jnp.int32, (CELLS, CELLS), 0)
    for j in range(LAYERS):
        y_cell = cell[j] & (CELLS - 1)
        spot = jnp.where(y_ids == y_cell, 1.0, 0.0).astype(BF16)
        values = rows_ref[j].reshape(4 * ROWS, CELLS)
        high = values.astype(BF16)
        low = (values - high.astype(F32)).astype(BF16)
        at_y = lax.dot_general(
            jnp.concatenate([high, low], axis=0), spot, (((1,), (1,)), ((), ())),
            preferred_element_type=F32,
        )
        rows_ref[j] = (at_y[: 4 * ROWS] + at_y[4 * ROWS :]).reshape(4, ROWS, CELLS)
    mix_rows(rows_ref, green_ref, pair_ref, fwd_ref, inv_ref, out_ref, spec_ref, kern_ref, mixed_ref)


def x_inverse(rows_ref, table_ref):
    parts = [
        jnp.concatenate(
            [rows_ref[:, 2 * p + c].reshape(WAVES, CELLS) for p in range(POLS)], axis=1
        )
        for c in range(2)
    ]
    waves = jnp.concatenate(parts, axis=0)
    cells = jnp.dot(table_ref[...], split_cat(waves, 0), preferred_element_type=F32)
    return [
        [cells[c * CELLS : (c + 1) * CELLS, p * CELLS : (p + 1) * CELLS] for c in range(2)]
        for p in range(POLS)
    ]


def residual_kernel(rows_ref, field_ref, station_ref, seen_ref, error_ref, table_ref, total_ref, sent_ref):
    scattered = x_inverse(rows_ref, table_ref)
    cell = station_ref[...]
    ids = lax.broadcasted_iota(jnp.int32, (CELLS, CELLS), 0)
    x_spot = jnp.where(ids == (cell >> 7), 1.0, 0.0).astype(BF16)
    y_spot = ids == (cell & (CELLS - 1))
    sent = []
    for p in range(POLS):
        weight = error_ref[0, p] * error_ref[0, p]
        for c in range(2):
            total = field_ref[0, p, c, 0] + scattered[p][c]
            total_ref[2 * p + c] = total
            turned = total.T
            picked = jnp.zeros((CELLS, CELLS), F32)
            for _ in range(3):
                piece = turned.astype(BF16)
                picked = picked + jnp.dot(piece, x_spot, preferred_element_type=F32)
                turned = turned - piece.astype(F32)
            predicted = jnp.sum(jnp.where(y_spot, picked, 0.0), axis=0, keepdims=True)
            resid = (predicted - seen_ref[0, p, c]) / weight
            sent.append(-resid if c else resid)
    sent.append(cell.astype(F32))
    sent.append(jnp.zeros((3, CELLS), F32))
    message = jnp.concatenate(sent, axis=0)
    sent_ref[...] = jnp.broadcast_to(message[None], (LAYERS, 8, CELLS))


def gradient_kernel(rows_ref, total_ref, table_ref, out_ref):
    adjoint = x_inverse(rows_ref, table_ref)
    term = jnp.zeros((CELLS, CELLS), F32)
    for p in range(POLS):
        term = term + (total_ref[2 * p] * adjoint[p][0] - total_ref[2 * p + 1] * adjoint[p][1])
    out_ref[...] = jnp.broadcast_to(term[None], (RING, CELLS, CELLS))


def call(kernel, out_shape, scratch=(), smem=0, operands=()):
    specs = [pl.BlockSpec(memory_space=pltpu.SMEM)] * smem
    specs += [pl.BlockSpec(memory_space=pltpu.VMEM)] * (len(operands) - smem)
    if isinstance(out_shape, list):
        out_specs = [pl.BlockSpec(memory_space=pltpu.VMEM)] * len(out_shape)
    else:
        out_specs = pl.BlockSpec(memory_space=pltpu.VMEM)
    return pl.pallas_call(
        kernel,
        out_shape=out_shape,
        in_specs=specs,
        out_specs=out_specs,
        scratch_shapes=list(scratch),
        compiler_params=pltpu.CompilerParams(vmem_limit_bytes=VMEM_BYTES),
    )(*operands)


def over_layers(values):
    return lax.all_to_all(values, "layer", split_axis=0, concat_axis=0, tiled=True)


def sum_over_freq(copies, size):
    rings = [list(range(r, r + RING)) for r in range(0, size, RING)]
    lines = [list(range(r, size, RING)) for r in range(RING)]
    for groups in (rings, lines):
        parts = lax.all_to_all(
            copies, "freq", split_axis=0, concat_axis=0, tiled=True, axis_index_groups=groups
        )
        total = (parts[0] + parts[1]) + (parts[2] + parts[3])
        copies = jnp.broadcast_to(total[None], copies.shape)
    return total


def per_device(conductivity, background, green, pair_table, stations, observed, data_error, freqs):
    x_fwd, y_fwd, y_inv, x_inv = dft_blocks()
    x_fwd, x_inv = left_table(x_fwd), left_table(x_inv)
    y_fwd, y_inv = right_table(y_fwd), right_table(y_inv)
    rows_shape = jax.ShapeDtypeStruct((LAYERS, 4, ROWS, CELLS), F32)
    scratch = (
        pltpu.VMEM((2, LAYERS, 3 * POLS, ROWS, CELLS), F32),
        pltpu.VMEM((2, green.shape[2], 3, ROWS, CELLS), F32),
        pltpu.VMEM((POLS, LAYERS, ROWS, 2 * WAVES), F32),
    )
    rows = call(x_forward_kernel, rows_shape, operands=(conductivity, background, x_fwd))
    back = call(
        mix_kernel, rows_shape, scratch, 1,
        (pair_table, over_layers(rows), green, y_fwd, y_inv),
    )
    total, sent = call(
        residual_kernel,
        [
            jax.ShapeDtypeStruct((4, CELLS, CELLS), F32),
            jax.ShapeDtypeStruct((LAYERS, 8, CELLS), F32),
        ],
        operands=(over_layers(back), background, stations, observed, data_error, x_inv),
    )
    first = (lax.axis_index("layer") * ROWS).astype(jnp.int32).reshape(1)
    back = call(
        adjoint_mix_kernel, rows_shape,
        (pltpu.VMEM((LAYERS, 4, ROWS, CELLS), F32),) + scratch, 2,
        (pair_table, first, over_layers(sent), green, y_fwd, y_inv),
    )
    copies = call(
        gradient_kernel,
        jax.ShapeDtypeStruct((RING, CELLS, CELLS), F32),
        operands=(over_layers(back), total, x_inv),
    )
    return sum_over_freq(copies, freqs)[None]


def solution(mesh):
    in_specs = (
        P("layer", None, None),
        P("freq", None, None, "layer", None, None),
        P("freq", None, None, "layer", None),
        P(),
        P("layer", None),
        P("freq", None, None, "layer", None),
        P("freq", None, "layer", None),
    )
    return jax.shard_map(
        functools.partial(per_device, freqs=mesh.shape["freq"]),
        mesh=mesh, in_specs=in_specs, out_specs=P("layer", None, None), check_vma=False,
    )
```

time: 633 us -> 149 us (0.24); the launches traced: 622 us -> 149 us
  waiting for transfers between devices: 291 us -> 13.3 us
  local copies, waits for them, and re-layouts: 144 us -> 2.99 us
  blocking collectives: 25.3 us -> 111 us
  other arithmetic: 70.3 us -> 0.66 us
  starting transfers between devices: 42.8 us -> 4.28 us
  matrix products: 32.3 us -> 0 us
  Pallas kernels: 0 us -> 16.1 us
  between operations: 14.3 us -> 0.15 us
    psum x1 -> x0, waiting for transfers between devices: 147 us -> none  [per_device(): return lax.psum(local_term, 'freq')]
    all_to_all x7 -> x1, waiting for transfers between devices: 144 us -> 13.3 us  [over_layers(): lax.all_to_all(values, 'layer', split_axis=0, concat_axis=0, tiled=True)]
    all_to_all x1 -> x5, blocking collectives: 25.3 us -> 111 us  [the longest x3 89.4 us: over_layers(): lax.all_to_all(values, 'layer', split_axis=0, concat_axis=0, tiled=True)]
    gather x130 -> x0, local copies, waits for them, and re-layouts: 79.9 us -> none  [the longest x64 37.5 us: one_receiver(): row_real = jnp.take(green_real, table_row, axis=0)]
    and x64 -> x0, other arithmetic: 44.6 us -> none  [one_receiver(): row_real = jnp.take(green_real, table_row, axis=0)]
    dynamic_update_slice x64 -> x0, local copies, waits for them, and re-layouts: 39.3 us -> none  [mix_layers(): mixed_real, mixed_imag = lax.map(one_receiver, pair_table)]
    all_to_all x7 -> x1, starting transfers between devices: 42.8 us -> 4.28 us  [over_layers(): lax.all_to_all(values, 'layer', split_axis=0, concat_axis=0, tiled=True)]
    dot_general x32 -> x0, matrix products: 32.3 us -> none  [the longest x2 2.57 us: inverse_rows(): jnp.einsum('kx,...ky->...xy', sine_table, im_part, precision=HIGHEST)]
  transfers between devices with their start and end apart: 8 -> 1, of which waited for: 8 -> 1; matrix products, arithmetic and copies ran while one was open for 1% -> 0% of each run, Pallas kernels for 0% -> 0%
where the time goes in v1:
time: 149 us
  blocking collectives  111 us (74%)
  Pallas kernels  16.1 us (11%)
  waiting for transfers between devices  13.3 us (9%)
  starting transfers between devices  4.28 us (3%)
  local copies, waits for them, and re-layouts  2.99 us (2%)
    all_to_all x3, blocking collectives, over_layers(): lax.all_to_all(values, 'layer', split_axis=0, concat_axis=0, tiled=True)  89.4 us
    all_to_all x2, blocking collectives, sum_over_freq(): lax.all_to_all(copies, 'freq', split_axis=0, concat_axis=0, tiled=True, a...  22.1 us
    pallas_call x5, Pallas kernels, call(): pl.pallas_call(kernel, out_shape=out_shape, in_specs=specs, out_specs=out...  16.1 us
    all_to_all x1, waiting for transfers between devices, over_layers(): lax.all_to_all(values, 'layer', split_axis=0, concat_axis=0, tiled=True)  13.3 us
    all_to_all x1, starting transfers between devices, over_layers(): lax.all_to_all(values, 'layer', split_axis=0, concat_axis=0, tiled=True)  4.28 us
  transfers between devices with their start and end apart: 1, of which 1 were waited for; matrix products, arithmetic and copies ran while one was open for 0% of the time, Pallas kernels for 0%

profile of v1, /device:TPU:8, one launch (start us, length us, event | category | flops | bytes accessed | tf_op | source)
XLA Modules:
  0.0 148.9 jit_solution(14758680621297572302)
XLA Ops:
  0.0 0.0 copy-start.4
  0.0 0.9 copy-done.4
  1.0 0.0 copy-start.6
  1.0 1.1 copy-done.6
  2.1 0.0 copy-start.8
  2.1 0.8 copy-done.8
  2.9 0.0 copy-start.2
  2.9 0.0 copy-start.3
  2.9 0.4 shard_map.109
  3.3 0.0 copy-start.1
  3.3 0.0 copy-start.7
  3.3 37.9 %all_to_all.30.rows_ref = f32[32,4,8,128]{3,2,1,0:T(8,128)S(1)} all-to-all(f32[32,4,8,128]{3,2,1,0:T(8,128)S(1)} %shard_map.109), channel_id=1, replica_groups=mesh['freq'=16,'layer'=32] {'layer'}, dimensions={0} | all-to-all | bytes 1048576 | tf_op jit(solution)/shard_map/all_to_all | solution.py:246
  41.2 0.0 copy-done.2
  41.2 0.0 copy-done.3
  41.2 0.0 copy-done.1
  41.3 0.0 copy-done.7
  41.3 0.0 copy-start.9
  41.3 0.0 copy-start.10
  41.3 0.0 copy-start.11
  41.3 6.6 %shard_map.110 = f32[32,4,8,128]{3,2,1,0:T(8,128)S(1)} custom-call(s32[32,32]{1,0:T(8,128)S(1)} %copy-done.7, f32[32,4,8,128]{3,2,1,0:T(8,128)S(1)} %all_to_all.30.rows_ref, f32[1,2,32,8,256]{4,3,2,1,0:T(8,128)S(1)} %copy-done.3, bf16[768,512]{1,0:T(8,128)(2,1)S(1)} %copy-done.2, bf16[1536,256]{1,0:T(8,128)(2,1)S(1)} %copy-done.1), custom_call_target="tpu_custom_call" | custom-call | tf_op jit(solution)/shard_map/pallas_call | solution.py:235
  47.9 0.0 copy-start
  47.9 0.0 copy-start.5
  47.9 25.5 %all_to_all.31.rows_ref = f32[32,4,8,128]{3,2,1,0:T(8,128)S(1)} all-to-all(f32[32,4,8,128]{3,2,1,0:T(8,128)S(1)} %shard_map.110), channel_id=1, replica_groups=mesh['freq'=16,'layer'=32] {'layer'}, dimensions={0} | all-to-all | bytes 1048576 | tf_op jit(solution)/shard_map/all_to_all | solution.py:246
  73.4 0.0 copy-done.9
  73.4 0.0 copy-done.10
  73.4 0.0 copy-done.11
  73.4 0.0 copy-done
  73.4 0.0 copy-done.5
  73.4 1.5 shard_map.111
  74.9 4.3 %all-to-all-start.2 = ((f32[32,8,128]{2,1,0:T(8,128)}), f32[32,8,128]{2,1,0:T(8,128)S(1)}, u32[]{:S(2)}, u32[]{:S(2)}) async-start(f32[32,8,128]{2,1,0:T(8,128)} %get-tuple-element.7), calls=%async_computation.2 | async-start | bytes 262144 | tf_op jit(solution)/shard_map/all_to_all | solution.py:246
  79.2 13.3 %all-to-all-done.2.sent_ref = f32[32,8,128]{2,1,0:T(8,128)S(1)} async-done(((f32[32,8,128]{2,1,0:T(8,128)}), f32[32,8,128]{2,1,0:T(8,128)S(1)}, u32[]{:S(2)}, u32[]{:S(2)}) %all-to-all-start.2) | async-done | bytes 131104 | tf_op jit(solution)/shard_map/all_to_all | solution.py:246
  92.6 7.3 %shard_map.112 = f32[32,4,8,128]{3,2,1,0:T(8,128)S(1)} custom-call(s32[32,32]{1,0:T(8,128)S(1)} %copy-done.7, s32[1]{0:T(128)} %bitcast.first_ref, f32[32,8,128]{2,1,0:T(8,128)S(1)} %all-to-all-done.2.sent_ref, f32[1,2,32,8,256]{4,3,2,1,0:T(8,128)S(1)} %copy-done.3, bf16[768,512]{1,0:T(8,128)(2,1)S(1)} %copy-done.2, bf16[1536,256]{1,0:T(8,128)(2,1)S(1)} %copy-done.1), custom_call_target="tpu_custom_call" | custom-call | tf_op jit(solution)/shard_map/pallas_call | solution.py:235
  99.8 26.0 %all_to_all.32.rows_ref = f32[32,4,8,128]{3,2,1,0:T(8,128)S(1)} all-to-all(f32[32,4,8,128]{3,2,1,0:T(8,128)S(1)} %shard_map.112), channel_id=1, replica_groups=mesh['freq'=16,'layer'=32] {'layer'}, dimensions={0} | all-to-all | bytes 1048576 | tf_op jit(solution)/shard_map/all_to_all | solution.py:246
  125.8 0.4 shard_map.113
  126.2 10.8 %all_to_all.33 = f32[4,128,128]{2,1,0:T(8,128)S(1)} all-to-all(f32[4,128,128]{2,1,0:T(8,128)S(1)} %shard_map.113), channel_id=1, replica_groups={{0,32,64,96},{128,160,192,224},{256,288,320,352},{384,416,448,480},{1,3..., dimensions={0} | all-to-all | bytes 524288 | tf_op jit(solution)/shard_map/all_to_all | solution.py:253
  137.0 11.3 %all_to_all.34 = f32[4,128,128]{2,1,0:T(8,128)S(1)} all-to-all(f32[4,128,128]{2,1,0:T(8,128)S(1)} %broadcast_in_dim.10), channel_id=1, replica_groups={{0,128,256,384},{32,160,288,416},{64,192,320,448},{96,224,352,480},{1,1..., dimensions={0} | all-to-all | bytes 524288 | tf_op jit(solution)/shard_map/all_to_all | solution.py:253
  148.3 0.6 fusion
  (2 shorter events, 0.0 us)
Async XLA Ops:
  0.0 0.9 copy-start.4
  1.0 1.1 copy-start.6
  2.1 0.8 copy-start.8
  2.9 38.3 %copy-start.2 = (bf16[768,512]{1,0:T(8,128)(2,1)S(1)}, bf16[768,512]{1,0:T(8,128)(2,1)}, u32[]{:S(2)}) copy-start(bf16[768,512]{1,0:T(8,128)(2,1)} %constant.15.clone.fwd_ref) | copy-start | bytes 2359300
  2.9 38.3 %copy-start.3 = (f32[1,2,32,8,256]{4,3,2,1,0:T(8,128)S(1)}, f32[1,2,32,8,256]{4,3,2,1,0:T(8,128)}, u32[]{:S(2)}) copy-start(f32[1,2,32,8,256]{4,3,2,1,0:T(8,128)} %green_ref.3) | copy-start | bytes 1572868
  3.3 37.9 %copy-start.1 = (bf16[1536,256]{1,0:T(8,128)(2,1)S(1)}, bf16[1536,256]{1,0:T(8,128)(2,1)}, u32[]{:S(2)}) copy-start(bf16[1536,256]{1,0:T(8,128)(2,1)} %constant.16.clone.inv_ref) | copy-start | bytes 2359300
  3.3 37.9 %copy-start.7 = (s32[32,32]{1,0:T(8,128)S(1)}, s32[32,32]{1,0:T(8,128)}, u32[]{:S(2)}) copy-start(s32[32,32]{1,0:T(8,128)} %pair_ref.3) | copy-start | bytes 12292
  41.3 32.1 %copy-start.9 = (f32[1,2,2,1,128]{4,3,2,1,0:T(1,128)S(1)}, f32[1,2,2,1,128]{4,3,2,1,0:T(1,128)}, u32[]{:S(2)}) copy-start(f32[1,2,2,1,128]{4,3,2,1,0:T(1,128)} %seen_ref.1) | copy-start | bytes 6148
  41.3 32.1 %copy-start.10 = (f32[1,2,1,128]{3,2,1,0:T(1,128)S(1)}, f32[1,2,1,128]{3,2,1,0:T(1,128)}, u32[]{:S(2)}) copy-start(f32[1,2,1,128]{3,2,1,0:T(1,128)} %error_ref.1) | copy-start | bytes 3076
  41.3 32.1 %copy-start.11 = (s32[1,128]{1,0:T(1,128)S(1)}, s32[1,128]{1,0:T(1,128)}, u32[]{:S(2)}) copy-start(s32[1,128]{1,0:T(1,128)} %station_ref.1) | copy-start | bytes 1540
  47.9 25.5 %copy-start = (bf16[256,1536]{1,0:T(8,128)(2,1)S(1)}, bf16[256,1536]{1,0:T(8,128)(2,1)}, u32[]{:S(2)}) copy-start(bf16[256,1536]{1,0:T(8,128)(2,1)} %constant.17.clone.table_ref) | copy-start | bytes 2359300
  47.9 25.5 %copy-start.5 = (f32[1,2,2,1,128,128]{5,4,3,2,1,0:T(8,128)S(1)}, f32[1,2,2,1,128,128]{5,4,3,2,1,0:T(8,128)}, u32[]{:S(2)}) copy-start(f32[1,2,2,1,128,128]{5,4,3,2,1,0:T(8,128)} %field_ref.3) | copy-start | bytes 786436
  74.9 17.6 %all-to-all-start.2 = ((f32[32,8,128]{2,1,0:T(8,128)}), f32[32,8,128]{2,1,0:T(8,128)S(1)}, u32[]{:S(2)}, u32[]{:S(2)}) async-start(f32[32,8,128]{2,1,0:T(8,128)} %get-tuple-element.7), calls=%async_computation.2 | async-start | bytes 262144 | tf_op jit(solution)/shard_map/all_to_all | solution.py:246

commit v2 on v1

--- a/solution.py
+++ b/solution.py
@@ -14,13 +14,15 @@
 WAVES = 256
 LAYERS = 32
 ROWS = 8
+KERNELS = 32
 POLS = 2
 GROUP = 4
-STEP = 8
+STEP = 16
 RING = 4
 F32 = jnp.float32
 BF16 = jnp.bfloat16
 VMEM_BYTES = 40 * 1024 * 1024
+FIRST_BYTES = 60 * 1024 * 1024
 
 
 def halves(table):
@@ -34,7 +36,7 @@
     cells = np.arange(CELLS)[None, :]
     angles = (waves * cells % WAVES) * (2.0 * math.pi / WAVES)
     cos, sin = np.cos(angles), np.sin(angles)
-    x_fwd = np.block([[cos, sin], [-sin, cos]])
+    x_fwd = np.concatenate(halves(np.concatenate([cos, sin], axis=1)), axis=1)
     y_fwd = np.block([[cos.T, -sin.T], [sin.T, cos.T]])
     y_inv = np.block([[cos, sin], [-sin, cos]]) / WAVES
     x_inv = np.block([[cos.T, -sin.T], [sin.T, cos.T]]) / WAVES
@@ -57,28 +59,46 @@
     return jnp.concatenate([high, low, high], axis=axis)
 
 
-def x_forward_kernel(cond_ref, field_ref, table_ref, out_ref):
+def x_forward_kernel(cond_hbm, field_hbm, table_hbm, out_ref, cond_ref, field_ref, table_ref, sems):
+    copies = [
+        pltpu.make_async_copy(source, target, sems.at[n])
+        for n, (source, target) in enumerate(
+            ((field_hbm, field_ref), (cond_hbm, cond_ref), (table_hbm, table_ref))
+        )
+    ]
+    for copy in copies:
+        copy.start()
+    copies[0].wait()
+    copies[1].wait()
     cond = cond_ref[0]
-    parts = [
-        jnp.concatenate([cond * field_ref[0, p, c, 0] for p in range(POLS)], axis=1)
-        for c in range(2)
+    high, low = [], []
+    for c in range(2):
+        part = jnp.concatenate([cond * field_ref[0, p, c, 0] for p in range(POLS)], axis=1)
+        high.append(part.astype(BF16))
+        low.append((part - high[c].astype(F32)).astype(BF16))
+    stacks = [
+        jnp.concatenate([jnp.concatenate([part[0], part[1]], axis=1), jnp.concatenate([part[1], -part[0]], axis=1)], axis=0)
+        for part in (high, low)
     ]
-    cells = jnp.concatenate(parts, axis=0)
-    rows = jnp.dot(table_ref[...], split_cat(cells, 0), preferred_element_type=F32)
-    for p in range(POLS):
-        for c in range(2):
-            block = rows[c * WAVES : (c + 1) * WAVES, p * CELLS : (p + 1) * CELLS]
-            out_ref[:, 2 * p + c] = block.reshape(LAYERS, ROWS, CELLS)
-
-
-def mix_rows(rows_ref, green_ref, pair_ref, fwd_ref, inv_ref, out_ref, spec_ref, kern_ref, mixed_ref):
+    cells = jnp.concatenate([stacks[0], stacks[1], stacks[0]], axis=0)
+    copies[2].wait()
+    table = table_ref[...]
+    table = jnp.concatenate([table[:, :WAVES], table], axis=1)
+    rows = jnp.dot(table, cells, preferred_element_type=F32)
+    for c in range(2):
+        for p in range(POLS):
+            at = (c * POLS + p) * CELLS
+            out_ref[:, 2 * p + c] = rows[:, at : at + CELLS].reshape(LAYERS, ROWS, CELLS)
+
+
+def mix_rows(rows_ref, green_ref, place_ref, fwd_ref, inv_ref, out_ref, spec_ref, kern_ref, mixed_ref):
+    lanes = [slice(h * CELLS, (h + 1) * CELLS) for h in range(2)]
     for h in range(2):
-        lanes = slice(h * CELLS, (h + 1) * CELLS)
-        g_re = green_ref[0, 0, :, :, lanes]
-        g_im = green_ref[0, 1, :, :, lanes]
-        kern_ref[h, :, 0] = g_re + g_im
-        kern_ref[h, :, 1] = g_re
-        kern_ref[h, :, 2] = g_im
+        g_re = green_ref[0, 0, :, :, lanes[h]]
+        g_im = green_ref[0, 1, :, :, lanes[h]]
+        kern_ref[h, :, 0:ROWS] = g_re + g_im
+        kern_ref[h, :, ROWS : 2 * ROWS] = g_re
+        kern_ref[h, :, 2 * ROWS :] = g_im
     for p in range(POLS):
         flat = [rows_ref[:, 2 * p + c].reshape(LAYERS * ROWS, CELLS) for c in range(2)]
         both = jnp.concatenate(flat, axis=1)
@@ -86,10 +106,11 @@
         for h in range(2):
             re = spec[:, h * CELLS : (h + 1) * CELLS].reshape(LAYERS, ROWS, CELLS)
             im = spec[:, WAVES + h * CELLS : WAVES + (h + 1) * CELLS].reshape(LAYERS, ROWS, CELLS)
-            spec_ref[h, :, 3 * p] = re
-            spec_ref[h, :, 3 * p + 1] = im - re
-            spec_ref[h, :, 3 * p + 2] = re + im
-
+            for k, value in enumerate((re, im - re, re + im)):
+                at = (3 * p + k) * ROWS
+                spec_ref[h, :, at : at + ROWS] = value
+
+    kern = [kern_ref.at[h].reshape(KERNELS * 3 * ROWS, CELLS) for h in range(2)]
     for h in range(2):
 
         def one_group(group, carry, h=h):
@@ -97,16 +118,18 @@
 
             def some_sources(chunk, sums):
                 sums = list(sums)
+                base = first * LAYERS + chunk * STEP
                 for s in range(STEP):
                     j = chunk * STEP + s
-                    src = [spec_ref[h, j, k] for k in range(3 * POLS)]
+                    src = [spec_ref[h, j, k * ROWS : (k + 1) * ROWS] for k in range(3 * POLS)]
                     for r in range(GROUP):
-                        n = pair_ref[first + r, j]
-                        kern = [kern_ref[h, n, k] for k in range(3)]
-                        for p in range(POLS):
-                            for k in range(3):
+                        place = place_ref[base + (r * LAYERS + s)]
+                        for k in range(3):
+                            row = pl.multiple_of(place + k * ROWS, ROWS)
+                            factor = kern[h][pl.ds(row, ROWS), :]
+                            for p in range(POLS):
                                 at = (r * POLS + p) * 3 + k
-                                sums[at] = sums[at] + kern[k] * src[3 * p + k]
+                                sums[at] = sums[at] + factor * src[3 * p + k]
                 return tuple(sums)
 
             zero = jnp.zeros((ROWS, CELLS), F32)
@@ -129,8 +152,8 @@
             out_ref[:, 2 * p + c] = back[:, c * CELLS : (c + 1) * CELLS].reshape(LAYERS, ROWS, CELLS)
 
 
-def mix_kernel(pair_ref, rows_ref, green_ref, fwd_ref, inv_ref, out_ref, spec_ref, kern_ref, mixed_ref):
-    mix_rows(rows_ref, green_ref, pair_ref, fwd_ref, inv_ref, out_ref, spec_ref, kern_ref, mixed_ref)
+def mix_kernel(place_ref, rows_ref, green_ref, fwd_ref, inv_ref, out_ref, spec_ref, kern_ref, mixed_ref):
+    mix_rows(rows_ref, green_ref, place_ref, fwd_ref, inv_ref, out_ref, spec_ref, kern_ref, mixed_ref)
 
 
 def sin_pi(v):
@@ -143,10 +166,11 @@
 
 
 def adjoint_mix_kernel(
-    pair_ref, first_ref, sent_ref, green_ref, fwd_ref, inv_ref,
+    place_ref, first_ref, sent_ref, green_ref, fwd_ref, inv_ref,
     out_ref, rows_ref, spec_ref, kern_ref, mixed_ref,
 ):
-    cell = sent_ref[:, 4:5, :].astype(jnp.int32)
+    sent = [sent_ref[:, :, k * CELLS : (k + 1) * CELLS] for k in range(5)]
+    cell = sent[4].astype(jnp.int32)
     x_cell = cell >> 7
     wave = first_ref[0] + lax.broadcasted_iota(jnp.int32, (LAYERS, ROWS, CELLS), 1)
     turn = (wave * x_cell) & (WAVES - 1)
@@ -156,8 +180,7 @@
     sin = sin_pi(jnp.minimum(size, 1.0 - size))
     sin = jnp.where(u < 0, sin, -sin)
     for p in range(POLS):
-        re = sent_ref[:, 2 * p : 2 * p + 1, :]
-        im = sent_ref[:, 2 * p + 1 : 2 * p + 2, :]
+        re, im = sent[2 * p], sent[2 * p + 1]
         rows_ref[:, 2 * p] = re * cos + im * sin
         rows_ref[:, 2 * p + 1] = im * cos - re * sin
     y_ids = lax.broadcasted_iota(jnp.int32, (CELLS, CELLS), 0)
@@ -172,7 +195,7 @@
             preferred_element_type=F32,
         )
         rows_ref[j] = (at_y[: 4 * ROWS] + at_y[4 * ROWS :]).reshape(4, ROWS, CELLS)
-    mix_rows(rows_ref, green_ref, pair_ref, fwd_ref, inv_ref, out_ref, spec_ref, kern_ref, mixed_ref)
+    mix_rows(rows_ref, green_ref, place_ref, fwd_ref, inv_ref, out_ref, spec_ref, kern_ref, mixed_ref)
 
 
 def x_inverse(rows_ref, table_ref):
@@ -212,9 +235,8 @@
             resid = (predicted - seen_ref[0, p, c]) / weight
             sent.append(-resid if c else resid)
     sent.append(cell.astype(F32))
-    sent.append(jnp.zeros((3, CELLS), F32))
-    message = jnp.concatenate(sent, axis=0)
-    sent_ref[...] = jnp.broadcast_to(message[None], (LAYERS, 8, CELLS))
+    message = jnp.concatenate(sent, axis=1)
+    sent_ref[...] = jnp.broadcast_to(message[None], (LAYERS, 1, 5 * CELLS))
 
 
 def gradient_kernel(rows_ref, total_ref, table_ref, out_ref):
@@ -260,24 +282,37 @@
 
 def per_device(conductivity, background, green, pair_table, stations, observed, data_error, freqs):
     x_fwd, y_fwd, y_inv, x_inv = dft_blocks()
-    x_fwd, x_inv = left_table(x_fwd), left_table(x_inv)
+    x_inv = left_table(x_inv)
     y_fwd, y_inv = right_table(y_fwd), right_table(y_inv)
+    places = (pair_table * (3 * ROWS)).reshape(-1)
     rows_shape = jax.ShapeDtypeStruct((LAYERS, 4, ROWS, CELLS), F32)
     scratch = (
-        pltpu.VMEM((2, LAYERS, 3 * POLS, ROWS, CELLS), F32),
-        pltpu.VMEM((2, green.shape[2], 3, ROWS, CELLS), F32),
+        pltpu.VMEM((2, LAYERS, 3 * POLS * ROWS, CELLS), F32),
+        pltpu.VMEM((2, KERNELS, 3 * ROWS, CELLS), F32),
         pltpu.VMEM((POLS, LAYERS, ROWS, 2 * WAVES), F32),
     )
-    rows = call(x_forward_kernel, rows_shape, operands=(conductivity, background, x_fwd))
+    rows = pl.pallas_call(
+        x_forward_kernel,
+        out_shape=rows_shape,
+        in_specs=[pl.BlockSpec(memory_space=pl.ANY)] * 3,
+        out_specs=pl.BlockSpec(memory_space=pltpu.VMEM),
+        scratch_shapes=[
+            pltpu.VMEM(conductivity.shape, F32),
+            pltpu.VMEM(background.shape, F32),
+            pltpu.VMEM(x_fwd.shape, BF16),
+            pltpu.SemaphoreType.DMA((3,)),
+        ],
+        compiler_params=pltpu.CompilerParams(vmem_limit_bytes=FIRST_BYTES),
+    )(conductivity, background, x_fwd)
     back = call(
         mix_kernel, rows_shape, scratch, 1,
-        (pair_table, over_layers(rows), green, y_fwd, y_inv),
+        (places, over_layers(rows), green, y_fwd, y_inv),
     )
     total, sent = call(
         residual_kernel,
         [
             jax.ShapeDtypeStruct((4, CELLS, CELLS), F32),
-            jax.ShapeDtypeStruct((LAYERS, 8, CELLS), F32),
+            jax.ShapeDtypeStruct((LAYERS, 1, 5 * CELLS), F32),
         ],
         operands=(over_layers(back), background, stations, observed, data_error, x_inv),
     )
@@ -285,7 +320,7 @@
     back = call(
         adjoint_mix_kernel, rows_shape,
         (pltpu.VMEM((LAYERS, 4, ROWS, CELLS), F32),) + scratch, 2,
-        (pair_table, first, over_layers(sent), green, y_fwd, y_inv),
+        (places, first, over_layers(sent), green, y_fwd, y_inv),
     )
     copies = call(
         gradient_kernel,

time: 149 us -> 145 us (0.973)
  blocking collectives: 111 us -> 73.5 us
  waiting for transfers between devices: 13.3 us -> 34 us
  starting transfers between devices: 4.28 us -> 20.6 us
  local copies, waits for them, and re-layouts: 2.99 us -> 0.14 us
    all_to_all x3 -> x2, blocking collectives: 89.4 us -> 51.5 us  [over_layers(): lax.all_to_all(values, 'layer', split_axis=0, concat_axis=0, tiled=True)]
    all_to_all x1 -> x2, waiting for transfers between devices: 13.3 us -> 34 us  [over_layers(): lax.all_to_all(values, 'layer', split_axis=0, concat_axis=0, tiled=True)]
    all_to_all x1 -> x2, starting transfers between devices: 4.28 us -> 20.6 us  [over_layers(): lax.all_to_all(values, 'layer', split_axis=0, concat_axis=0, tiled=True)]
    unnamed x24 -> x18, local copies, waits for them, and re-layouts: 2.97 us -> 0.05 us
    pallas_call x5 -> x4, Pallas kernels: 16.1 us -> 13.6 us  [call(): pl.pallas_call(kernel, out_shape=out_shape, in_specs=specs, out_specs=out...]
    pallas_call x0 -> x1, Pallas kernels: none -> 2.35 us  [per_device(): pl.pallas_call(x_forward_kernel, out_shape=rows_shape, in_specs=[pl.Block...]
  transfers between devices with their start and end apart: 1 -> 2, of which waited for: 1 -> 2; matrix products, arithmetic and copies ran while one was open for 0% -> 0% of each run, Pallas kernels for 0% -> 0%
where the time goes in v2:
time: 145 us
  blocking collectives  73.5 us (51%)
  waiting for transfers between devices  34 us (23%)
  starting transfers between devices  20.6 us (14%)
  Pallas kernels  16 us (11%)
    all_to_all x2, blocking collectives, over_layers(): lax.all_to_all(values, 'layer', split_axis=0, concat_axis=0, tiled=True)  51.5 us
    all_to_all x2, waiting for transfers between devices, over_layers(): lax.all_to_all(values, 'layer', split_axis=0, concat_axis=0, tiled=True)  34 us
    all_to_all x2, blocking collectives, sum_over_freq(): lax.all_to_all(copies, 'freq', split_axis=0, concat_axis=0, tiled=True, a...  22.1 us
    all_to_all x2, starting transfers between devices, over_layers(): lax.all_to_all(values, 'layer', split_axis=0, concat_axis=0, tiled=True)  20.6 us
    pallas_call x4, Pallas kernels, call(): pl.pallas_call(kernel, out_shape=out_shape, in_specs=specs, out_specs=out...  13.6 us
  transfers between devices with their start and end apart: 2, of which 2 were waited for; matrix products, arithmetic and copies ran while one was open for 0% of the time, Pallas kernels for 0%

profile of v2, /device:TPU:8, one launch (start us, length us, event | category | flops | bytes accessed | tf_op | source)
XLA Modules:
  0.0 145.1 jit_solution(13477433026547145912)
XLA Ops:
  0.0 0.0 copy-start.2
  0.0 0.0 copy-start.3
  0.0 2.4 %shard_map.109 = f32[32,4,8,128]{3,2,1,0:T(8,128)} custom-call(f32[1,128,128]{2,1,0:T(8,128)} %cond_hbm.1, f32[1,2,2,1,128,128]{5,4,3,2,1,0:T(8,128)} %field_ref.1, bf16[256,512]{1,0:T(8,128)(2,1)} %constant.16.clone.table_hbm), custom_call_target="tpu_custom_call" | custom-call | tf_op jit(solution)/shard_map/pallas_call | solution.py:294
  2.4 0.0 copy-start.8
  2.4 0.0 copy-start.1
  2.4 16.3 %all-to-all-start = ((f32[32,4,8,128]{3,2,1,0:T(8,128)}), f32[32,4,8,128]{3,2,1,0:T(8,128)S(1)}, u32[]{:S(2)}, u32[]{:S(2)}) async-start(f32[32,4,8,128]{3,2,1,0:T(8,128)} %shard_map.109), calls=%async_computation | async-start | bytes 1048576 | tf_op jit(solution)/shard_map/all_to_all | solution.py:268
  18.7 0.0 copy-done.8
  18.7 0.1 reshape.6.place_ref
  18.8 21.7 %all-to-all-done.rows_ref = f32[32,4,8,128]{3,2,1,0:T(8,128)S(1)} async-done(((f32[32,4,8,128]{3,2,1,0:T(8,128)}), f32[32,4,8,128]{3,2,1,0:T(8,128)S(1)}, u32[]{:S(2)}, u32[]{:S(2)}) %all-to-all-start) | async-done | bytes 524320 | tf_op jit(solution)/shard_map/all_to_all | solution.py:268
  40.5 0.0 copy-done.2
  40.5 0.0 copy-done.3
  40.5 0.0 copy-done.1
  40.5 0.0 copy-start.5
  40.5 0.0 copy-start.6
  40.6 0.0 copy-start.7
  40.6 5.6 %shard_map.110 = f32[32,4,8,128]{3,2,1,0:T(8,128)S(1)} custom-call(s32[1024]{0:T(1024)S(1)} %reshape.6.place_ref, f32[32,4,8,128]{3,2,1,0:T(8,128)S(1)} %all-to-all-done.rows_ref, f32[1,2,32,8,256]{4,3,2,1,0:T(8,128)S(1)} %copy-done.3, bf16[768,512]{1,0:T(8,128)(2,1)S(1)} %copy-done.2, bf16[1536,256]{1,0:T(8,128)(2,1)S(1)} %copy-done.1), custom_call_target="tpu_custom_call" | custom-call | tf_op jit(solution)/shard_map/pallas_call | solution.py:257
  46.1 0.0 copy-start
  46.2 0.0 copy-start.4
  46.2 25.5 %all_to_all.30.rows_ref = f32[32,4,8,128]{3,2,1,0:T(8,128)S(1)} all-to-all(f32[32,4,8,128]{3,2,1,0:T(8,128)S(1)} %shard_map.110), channel_id=1, replica_groups=mesh['freq'=16,'layer'=32] {'layer'}, dimensions={0} | all-to-all | bytes 1048576 | tf_op jit(solution)/shard_map/all_to_all | solution.py:268
  71.6 0.0 copy-done.5
  71.6 0.0 copy-done.6
  71.6 0.0 copy-done.7
  71.6 0.0 copy-done
  71.7 0.0 copy-done.4
  71.7 1.5 %shard_map.111 = (f32[4,128,128]{2,1,0:T(8,128)S(1)}, f32[32,1,640]{2,1,0:T(1,128)}) custom-call(f32[32,4,8,128]{3,2,1,0:T(8,128)S(1)} %all_to_all.30.rows_ref, f32[1,2,2,1,128,128]{5,4,3,2,1,0:T(8,128)S(1)} %copy-done.4, s32[1,128]{1,0:T(1,128)S(1)} %copy-done.7, f32[1,2,2,1,128]{4,3,2,1,0:T(1,128)S(1)} %copy-done.5, f32[1,2,1,128]{3,2,1,0:T(1,128)S(1)} %copy-done.6, ...), custom_call_target="tpu_custom_call" | custom-call | tf_op jit(solution)/shard_map/pallas_call | solution.py:257
  73.1 4.3 %all-to-all-start.2 = ((f32[32,1,640]{2,1,0:T(1,128)}), f32[32,1,640]{2,1,0:T(1,128)S(1)}, u32[]{:S(2)}, u32[]{:S(2)}) async-start(f32[32,1,640]{2,1,0:T(1,128)} %get-tuple-element.7), calls=%async_computation.2 | async-start | bytes 163840 | tf_op jit(solution)/shard_map/all_to_all | solution.py:268
  77.4 12.3 %all-to-all-done.2.sent_ref = f32[32,1,640]{2,1,0:T(1,128)S(1)} async-done(((f32[32,1,640]{2,1,0:T(1,128)}), f32[32,1,640]{2,1,0:T(1,128)S(1)}, u32[]{:S(2)}, u32[]{:S(2)}) %all-to-all-start.2) | async-done | bytes 81952 | tf_op jit(solution)/shard_map/all_to_all | solution.py:268
  89.7 6.2 %shard_map.112 = f32[32,4,8,128]{3,2,1,0:T(8,128)S(1)} custom-call(s32[1024]{0:T(1024)S(1)} %reshape.6.place_ref, s32[1]{0:T(128)} %bitcast.first_ref, f32[32,1,640]{2,1,0:T(1,128)S(1)} %all-to-all-done.2.sent_ref, f32[1,2,32,8,256]{4,3,2,1,0:T(8,128)S(1)} %copy-done.3, bf16[768,512]{1,0:T(8,128)(2,1)S(1)} %copy-done.2, bf16[1536,256]{1,0:T(8,128)(2,1)S(1)} %copy-done.1), custom_call_target="tpu_custom_call" | custom-call | tf_op jit(solution)/shard_map/pallas_call | solution.py:257
  96.0 26.0 %all_to_all.31.rows_ref = f32[32,4,8,128]{3,2,1,0:T(8,128)S(1)} all-to-all(f32[32,4,8,128]{3,2,1,0:T(8,128)S(1)} %shard_map.112), channel_id=1, replica_groups=mesh['freq'=16,'layer'=32] {'layer'}, dimensions={0} | all-to-all | bytes 1048576 | tf_op jit(solution)/shard_map/all_to_all | solution.py:268
  121.9 0.4 shard_map.113
  122.3 10.8 %all_to_all.32 = f32[4,128,128]{2,1,0:T(8,128)S(1)} all-to-all(f32[4,128,128]{2,1,0:T(8,128)S(1)} %shard_map.113), channel_id=1, replica_groups={{0,32,64,96},{128,160,192,224},{256,288,320,352},{384,416,448,480},{1,3..., dimensions={0} | all-to-all | bytes 524288 | tf_op jit(solution)/shard_map/all_to_all | solution.py:275
  133.1 11.3 %all_to_all.33 = f32[4,128,128]{2,1,0:T(8,128)S(1)} all-to-all(f32[4,128,128]{2,1,0:T(8,128)S(1)} %broadcast_in_dim.10), channel_id=1, replica_groups={{0,128,256,384},{32,160,288,416},{64,192,320,448},{96,224,352,480},{1,1..., dimensions={0} | all-to-all | bytes 524288 | tf_op jit(solution)/shard_map/all_to_all | solution.py:275
  144.4 0.6 fusion
  (3 shorter events, 0.0 us)
Async XLA Ops:
  0.0 40.5 %copy-start.2 = (bf16[768,512]{1,0:T(8,128)(2,1)S(1)}, bf16[768,512]{1,0:T(8,128)(2,1)}, u32[]{:S(2)}) copy-start(bf16[768,512]{1,0:T(8,128)(2,1)} %constant.17.clone.fwd_ref) | copy-start | bytes 2359300
  0.0 40.5 %copy-start.3 = (f32[1,2,32,8,256]{4,3,2,1,0:T(8,128)S(1)}, f32[1,2,32,8,256]{4,3,2,1,0:T(8,128)}, u32[]{:S(2)}) copy-start(f32[1,2,32,8,256]{4,3,2,1,0:T(8,128)} %green_ref.3) | copy-start | bytes 1572868
  2.4 16.3 %copy-start.8 = (s32[32,32]{1,0:T(8,128)S(1)}, s32[32,32]{1,0:T(8,128)}, u32[]{:S(2)}) copy-start(s32[32,32]{1,0:T(8,128)} %param.14) | copy-start | bytes 12292
  2.4 38.2 %copy-start.1 = (bf16[1536,256]{1,0:T(8,128)(2,1)S(1)}, bf16[1536,256]{1,0:T(8,128)(2,1)}, u32[]{:S(2)}) copy-start(bf16[1536,256]{1,0:T(8,128)(2,1)} %constant.18.clone.inv_ref) | copy-start | bytes 2359300
  2.4 38.1 %all-to-all-start = ((f32[32,4,8,128]{3,2,1,0:T(8,128)}), f32[32,4,8,128]{3,2,1,0:T(8,128)S(1)}, u32[]{:S(2)}, u32[]{:S(2)}) async-start(f32[32,4,8,128]{3,2,1,0:T(8,128)} %shard_map.109), calls=%async_computation | async-start | bytes 1048576 | tf_op jit(solution)/shard_map/all_to_all | solution.py:268
  40.5 31.1 %copy-start.5 = (f32[1,2,2,1,128]{4,3,2,1,0:T(1,128)S(1)}, f32[1,2,2,1,128]{4,3,2,1,0:T(1,128)}, u32[]{:S(2)}) copy-start(f32[1,2,2,1,128]{4,3,2,1,0:T(1,128)} %seen_ref.1) | copy-start | bytes 6148
  40.5 31.1 %copy-start.6 = (f32[1,2,1,128]{3,2,1,0:T(1,128)S(1)}, f32[1,2,1,128]{3,2,1,0:T(1,128)}, u32[]{:S(2)}) copy-start(f32[1,2,1,128]{3,2,1,0:T(1,128)} %error_ref.1) | copy-start | bytes 3076
  40.6 31.1 %copy-start.7 = (s32[1,128]{1,0:T(1,128)S(1)}, s32[1,128]{1,0:T(1,128)}, u32[]{:S(2)}) copy-start(s32[1,128]{1,0:T(1,128)} %station_ref.1) | copy-start | bytes 1540
  46.1 25.5 %copy-start = (bf16[256,1536]{1,0:T(8,128)(2,1)S(1)}, bf16[256,1536]{1,0:T(8,128)(2,1)}, u32[]{:S(2)}) copy-start(bf16[256,1536]{1,0:T(8,128)(2,1)} %constant.19.clone.table_ref) | copy-start | bytes 2359300
  46.2 25.5 %copy-start.4 = (f32[1,2,2,1,128,128]{5,4,3,2,1,0:T(8,128)S(1)}, f32[1,2,2,1,128,128]{5,4,3,2,1,0:T(8,128)}, u32[]{:S(2)}) copy-start(f32[1,2,2,1,128,128]{5,4,3,2,1,0:T(8,128)} %field_ref.1) | copy-start | bytes 786436
  73.1 16.6 %all-to-all-start.2 = ((f32[32,1,640]{2,1,0:T(1,128)}), f32[32,1,640]{2,1,0:T(1,128)S(1)}, u32[]{:S(2)}, u32[]{:S(2)}) async-start(f32[32,1,640]{2,1,0:T(1,128)} %get-tuple-element.7), calls=%async_computation.2 | async-start | bytes 163840 | tf_op jit(solution)/shard_map/all_to_all | solution.py:268

commit v3 on v2

--- a/solution.py
+++ b/solution.py
@@ -59,7 +59,10 @@
     return jnp.concatenate([high, low, high], axis=axis)
 
 
-def x_forward_kernel(cond_hbm, field_hbm, table_hbm, out_ref, cond_ref, field_ref, table_ref, sems):
+def x_forward_kernel(
+    cond_hbm, field_hbm, table_hbm, place_any, first_any, out_ref, cond_ref, field_ref, table_ref, sems
+):
+    del place_any, first_any
     copies = [
         pltpu.make_async_copy(source, target, sems.at[n])
         for n, (source, target) in enumerate(
@@ -285,6 +288,7 @@
     x_inv = left_table(x_inv)
     y_fwd, y_inv = right_table(y_fwd), right_table(y_inv)
     places = (pair_table * (3 * ROWS)).reshape(-1)
+    first = (lax.axis_index("layer") * ROWS).astype(jnp.int32).reshape(1)
     rows_shape = jax.ShapeDtypeStruct((LAYERS, 4, ROWS, CELLS), F32)
     scratch = (
         pltpu.VMEM((2, LAYERS, 3 * POLS * ROWS, CELLS), F32),
@@ -294,7 +298,8 @@
     rows = pl.pallas_call(
         x_forward_kernel,
         out_shape=rows_shape,
-        in_specs=[pl.BlockSpec(memory_space=pl.ANY)] * 3,
+        in_specs=[pl.BlockSpec(memory_space=pltpu.HBM)] * 3
+        + [pl.BlockSpec(memory_space=pl.ANY)] * 2,
         out_specs=pl.BlockSpec(memory_space=pltpu.VMEM),
         scratch_shapes=[
             pltpu.VMEM(conductivity.shape, F32),
@@ -303,7 +308,7 @@
             pltpu.SemaphoreType.DMA((3,)),
         ],
         compiler_params=pltpu.CompilerParams(vmem_limit_bytes=FIRST_BYTES),
-    )(conductivity, background, x_fwd)
+    )(conductivity, background, x_fwd, places, first)
     back = call(
         mix_kernel, rows_shape, scratch, 1,
         (places, over_layers(rows), green, y_fwd, y_inv),
@@ -316,7 +321,6 @@
         ],
         operands=(over_layers(back), background, stations, observed, data_error, x_inv),
     )
-    first = (lax.axis_index("layer") * ROWS).astype(jnp.int32).reshape(1)
     back = call(
         adjoint_mix_kernel, rows_shape,
         (pltpu.VMEM((LAYERS, 4, ROWS, CELLS), F32),) + scratch, 2,

time: 145 us -> 145 us (level)
  blocking collectives: 73.5 us -> 127 us
  waiting for transfers between devices: 34 us -> 0 us
  starting transfers between devices: 20.6 us -> 0 us
    all_to_all x2 -> x4, blocking collectives: 51.5 us -> 105 us  [over_layers(): lax.all_to_all(values, 'layer', split_axis=0, concat_axis=0, tiled=True)]
    all_to_all x2 -> x0, waiting for transfers between devices: 34 us -> none  [over_layers(): lax.all_to_all(values, 'layer', split_axis=0, concat_axis=0, tiled=True)]
    all_to_all x2 -> x0, starting transfers between devices: 20.6 us -> none  [over_layers(): lax.all_to_all(values, 'layer', split_axis=0, concat_axis=0, tiled=True)]
  transfers between devices with their start and end apart: 2 -> 0, of which waited for: 2 -> 0; matrix products, arithmetic and copies ran while one was open for 0% -> 0% of each run, Pallas kernels for 0% -> 0%
where the time goes in v3:
time: 145 us
  blocking collectives  127 us (88%)
  Pallas kernels  15.4 us (11%)
    all_to_all x4, blocking collectives, over_layers(): lax.all_to_all(values, 'layer', split_axis=0, concat_axis=0, tiled=True)  105 us
    all_to_all x2, blocking collectives, sum_over_freq(): lax.all_to_all(copies, 'freq', split_axis=0, concat_axis=0, tiled=True, a...  22.1 us
    pallas_call x4, Pallas kernels, call(): pl.pallas_call(kernel, out_shape=out_shape, in_specs=specs, out_specs=out...  13 us

profile of v3, /device:TPU:8, one launch (start us, length us, event | category | flops | bytes accessed | tf_op | source)
XLA Modules:
  0.0 145.0 jit_solution(4587229262193999576)
XLA Ops:
  0.0 0.7 broadcast_multiply_fusion
  0.7 0.7 reshape.6.place_any.place_ref
  1.4 0.0 copy-start.2
  1.4 0.0 copy-start.3
  1.4 2.4 %shard_map.109 = f32[32,4,8,128]{3,2,1,0:T(8,128)} custom-call(f32[1,128,128]{2,1,0:T(8,128)} %cond_hbm.1, f32[1,2,2,1,128,128]{5,4,3,2,1,0:T(8,128)} %field_ref.1, bf16[256,512]{1,0:T(8,128)(2,1)} %constant.16.clone.table_hbm, s32[1024]{0:T(1024)} %reshape.6.place_any.place_ref, s32[1]{0:T(128)} %bitcast.first_any.first_ref), custom_call_target="tpu_custom_call" | custom-call | tf_op jit(solution)/shard_map/pallas_call | solution.py:298
  3.8 0.0 copy-start.1
  3.8 0.0 copy-start.5
  3.8 38.1 %all_to_all.30.rows_ref = f32[32,4,8,128]{3,2,1,0:T(8,128)S(1)} all-to-all(f32[32,4,8,128]{3,2,1,0:T(8,128)} %shard_map.109), channel_id=1, replica_groups=mesh['freq'=16,'layer'=32] {'layer'}, dimensions={0} | all-to-all | bytes 1048576 | tf_op jit(solution)/shard_map/all_to_all | solution.py:271
  41.9 0.0 copy-done.2
  41.9 0.0 copy-done.3
  41.9 0.0 copy-done.1
  41.9 0.0 copy-done.5
  41.9 0.0 copy-start.6
  41.9 0.0 copy-start.7
  41.9 0.0 copy-start.8
  42.0 5.6 %shard_map.110 = f32[32,4,8,128]{3,2,1,0:T(8,128)S(1)} custom-call(s32[1024]{0:T(1024)S(1)} %copy-done.5, f32[32,4,8,128]{3,2,1,0:T(8,128)S(1)} %all_to_all.30.rows_ref, f32[1,2,32,8,256]{4,3,2,1,0:T(8,128)S(1)} %copy-done.3, bf16[768,512]{1,0:T(8,128)(2,1)S(1)} %copy-done.2, bf16[1536,256]{1,0:T(8,128)(2,1)S(1)} %copy-done.1), custom_call_target="tpu_custom_call" | custom-call | tf_op jit(solution)/shard_map/pallas_call | solution.py:260
  47.5 0.0 copy-start
  47.6 0.0 copy-start.4
  47.6 25.5 %all_to_all.31.rows_ref = f32[32,4,8,128]{3,2,1,0:T(8,128)S(1)} all-to-all(f32[32,4,8,128]{3,2,1,0:T(8,128)S(1)} %shard_map.110), channel_id=1, replica_groups=mesh['freq'=16,'layer'=32] {'layer'}, dimensions={0} | all-to-all | bytes 1048576 | tf_op jit(solution)/shard_map/all_to_all | solution.py:271
  73.0 0.0 copy-done.6
  73.0 0.0 copy-done.7
  73.0 0.0 copy-done.8
  73.1 0.0 copy-done
  73.1 0.0 copy-done.4
  73.1 0.8 shard_map.111
  73.9 15.7 %all_to_all.32.sent_ref = f32[32,1,640]{2,1,0:T(1,128)S(1)} all-to-all(f32[32,1,640]{2,1,0:T(1,128)S(1)} %get-tuple-element.7), channel_id=1, replica_groups=mesh['freq'=16,'layer'=32] {'layer'}, dimensions={0} | all-to-all | bytes 163840 | tf_op jit(solution)/shard_map/all_to_all | solution.py:271
  89.6 6.2 %shard_map.112 = f32[32,4,8,128]{3,2,1,0:T(8,128)S(1)} custom-call(s32[1024]{0:T(1024)S(1)} %copy-done.5, s32[1]{0:T(128)} %bitcast.first_any.first_ref, f32[32,1,640]{2,1,0:T(1,128)S(1)} %all_to_all.32.sent_ref, f32[1,2,32,8,256]{4,3,2,1,0:T(8,128)S(1)} %copy-done.3, bf16[768,512]{1,0:T(8,128)(2,1)S(1)} %copy-done.2, bf16[1536,256]{1,0:T(8,128)(2,1)S(1)} %copy-done.1), custom_call_target="tpu_custom_call" | custom-call | tf_op jit(solution)/shard_map/pallas_call | solution.py:260
  95.8 26.0 %all_to_all.33.rows_ref = f32[32,4,8,128]{3,2,1,0:T(8,128)S(1)} all-to-all(f32[32,4,8,128]{3,2,1,0:T(8,128)S(1)} %shard_map.112), channel_id=1, replica_groups=mesh['freq'=16,'layer'=32] {'layer'}, dimensions={0} | all-to-all | bytes 1048576 | tf_op jit(solution)/shard_map/all_to_all | solution.py:271
  121.8 0.4 shard_map.113
  122.2 10.8 %all_to_all.34 = f32[4,128,128]{2,1,0:T(8,128)S(1)} all-to-all(f32[4,128,128]{2,1,0:T(8,128)S(1)} %shard_map.113), channel_id=1, replica_groups={{0,32,64,96},{128,160,192,224},{256,288,320,352},{384,416,448,480},{1,3..., dimensions={0} | all-to-all | bytes 524288 | tf_op jit(solution)/shard_map/all_to_all | solution.py:278
  133.0 11.3 %all_to_all.35 = f32[4,128,128]{2,1,0:T(8,128)S(1)} all-to-all(f32[4,128,128]{2,1,0:T(8,128)S(1)} %broadcast_in_dim.10), channel_id=1, replica_groups={{0,128,256,384},{32,160,288,416},{64,192,320,448},{96,224,352,480},{1,1..., dimensions={0} | all-to-all | bytes 524288 | tf_op jit(solution)/shard_map/all_to_all | solution.py:278
  144.3 0.6 fusion
  (2 shorter events, 0.0 us)
Async XLA Ops:
  1.4 40.5 %copy-start.2 = (bf16[768,512]{1,0:T(8,128)(2,1)S(1)}, bf16[768,512]{1,0:T(8,128)(2,1)}, u32[]{:S(2)}) copy-start(bf16[768,512]{1,0:T(8,128)(2,1)} %constant.17.clone.fwd_ref) | copy-start | bytes 2359300
  1.4 40.5 %copy-start.3 = (f32[1,2,32,8,256]{4,3,2,1,0:T(8,128)S(1)}, f32[1,2,32,8,256]{4,3,2,1,0:T(8,128)}, u32[]{:S(2)}) copy-start(f32[1,2,32,8,256]{4,3,2,1,0:T(8,128)} %green_ref.3) | copy-start | bytes 1572868
  3.8 38.2 %copy-start.1 = (bf16[1536,256]{1,0:T(8,128)(2,1)S(1)}, bf16[1536,256]{1,0:T(8,128)(2,1)}, u32[]{:S(2)}) copy-start(bf16[1536,256]{1,0:T(8,128)(2,1)} %constant.18.clone.inv_ref) | copy-start | bytes 2359300
  3.8 38.1 %copy-start.5 = (s32[1024]{0:T(1024)S(1)}, s32[1024]{0:T(1024)}, u32[]{:S(2)}) copy-start(s32[1024]{0:T(1024)} %reshape.6.place_any.place_ref) | copy-start | bytes 12292
  41.9 31.1 %copy-start.6 = (f32[1,2,2,1,128]{4,3,2,1,0:T(1,128)S(1)}, f32[1,2,2,1,128]{4,3,2,1,0:T(1,128)}, u32[]{:S(2)}) copy-start(f32[1,2,2,1,128]{4,3,2,1,0:T(1,128)} %seen_ref.1) | copy-start | bytes 6148
  41.9 31.1 %copy-start.7 = (f32[1,2,1,128]{3,2,1,0:T(1,128)S(1)}, f32[1,2,1,128]{3,2,1,0:T(1,128)}, u32[]{:S(2)}) copy-start(f32[1,2,1,128]{3,2,1,0:T(1,128)} %error_ref.1) | copy-start | bytes 3076
  41.9 31.1 %copy-start.8 = (s32[1,128]{1,0:T(1,128)S(1)}, s32[1,128]{1,0:T(1,128)}, u32[]{:S(2)}) copy-start(s32[1,128]{1,0:T(1,128)} %station_ref.1) | copy-start | bytes 1540
  47.5 25.5 %copy-start = (bf16[256,1536]{1,0:T(8,128)(2,1)S(1)}, bf16[256,1536]{1,0:T(8,128)(2,1)}, u32[]{:S(2)}) copy-start(bf16[256,1536]{1,0:T(8,128)(2,1)} %constant.19.clone.table_ref) | copy-start | bytes 2359300
  47.6 25.5 %copy-start.4 = (f32[1,2,2,1,128,128]{5,4,3,2,1,0:T(8,128)S(1)}, f32[1,2,2,1,128,128]{5,4,3,2,1,0:T(8,128)}, u32[]{:S(2)}) copy-start(f32[1,2,2,1,128,128]{5,4,3,2,1,0:T(8,128)} %field_ref.1) | copy-start | bytes 786436

commit v4 on v3

--- a/solution.py
+++ b/solution.py
@@ -36,21 +36,19 @@
     cells = np.arange(CELLS)[None, :]
     angles = (waves * cells % WAVES) * (2.0 * math.pi / WAVES)
     cos, sin = np.cos(angles), np.sin(angles)
-    x_fwd = np.concatenate(halves(np.concatenate([cos, sin], axis=1)), axis=1)
+    x_fwd = np.concatenate([cos, sin], axis=1)
     y_fwd = np.block([[cos.T, -sin.T], [sin.T, cos.T]])
     y_inv = np.block([[cos, sin], [-sin, cos]]) / WAVES
     x_inv = np.block([[cos.T, -sin.T], [sin.T, cos.T]]) / WAVES
-    return x_fwd, y_fwd, y_inv, x_inv
-
-
-def left_table(table):
-    high, low = halves(table)
-    return np.concatenate([high, high, low], axis=1)
-
-
-def right_table(table):
-    high, low = halves(table)
-    return np.concatenate([high, high, low], axis=0)
+    y_both = np.concatenate(
+        [np.concatenate(halves(y_fwd), axis=0), np.concatenate(halves(y_inv), axis=1)], axis=0
+    )
+    return np.concatenate(halves(x_fwd), axis=1), y_both, np.concatenate(halves(x_inv), axis=1)
+
+
+def thrice(table, axis):
+    high, low = jnp.split(table, 2, axis=axis)
+    return jnp.concatenate([high, high, low], axis=axis)
 
 
 def split_cat(values, axis):
@@ -60,14 +58,14 @@
 
 
 def x_forward_kernel(
-    cond_hbm, field_hbm, table_hbm, place_any, first_any, out_ref, cond_ref, field_ref, table_ref, sems
+    cond_hbm, field_hbm, table_hbm, pair_hbm, first_any,
+    out_ref, place_ref, cond_ref, field_ref, table_ref, pair_ref, sems,
 ):
-    del place_any, first_any
+    del first_any
+    moves = ((field_hbm, field_ref), (cond_hbm, cond_ref), (table_hbm, table_ref), (pair_hbm, pair_ref))
     copies = [
         pltpu.make_async_copy(source, target, sems.at[n])
-        for n, (source, target) in enumerate(
-            ((field_hbm, field_ref), (cond_hbm, cond_ref), (table_hbm, table_ref))
-        )
+        for n, (source, target) in enumerate(moves)
     ]
     for copy in copies:
         copy.start()
@@ -84,17 +82,17 @@
         for part in (high, low)
     ]
     cells = jnp.concatenate([stacks[0], stacks[1], stacks[0]], axis=0)
+    copies[3].wait()
+    place_ref[...] = pair_ref[...] * (3 * ROWS)
     copies[2].wait()
-    table = table_ref[...]
-    table = jnp.concatenate([table[:, :WAVES], table], axis=1)
-    rows = jnp.dot(table, cells, preferred_element_type=F32)
+    rows = jnp.dot(thrice(table_ref[...], 1), cells, preferred_element_type=F32)
     for c in range(2):
         for p in range(POLS):
             at = (c * POLS + p) * CELLS
             out_ref[:, 2 * p + c] = rows[:, at : at + CELLS].reshape(LAYERS, ROWS, CELLS)
 
 
-def mix_rows(rows_ref, green_ref, place_ref, fwd_ref, inv_ref, out_ref, spec_ref, kern_ref, mixed_ref):
+def mix_rows(rows_ref, green_ref, place_ref, table_ref, out_ref, spec_ref, kern_ref, mixed_ref):
     lanes = [slice(h * CELLS, (h + 1) * CELLS) for h in range(2)]
     for h in range(2):
         g_re = green_ref[0, 0, :, :, lanes[h]]
@@ -102,10 +100,11 @@
         kern_ref[h, :, 0:ROWS] = g_re + g_im
         kern_ref[h, :, ROWS : 2 * ROWS] = g_re
         kern_ref[h, :, 2 * ROWS :] = g_im
+    forward = thrice(table_ref[: 2 * WAVES], 0)
     for p in range(POLS):
         flat = [rows_ref[:, 2 * p + c].reshape(LAYERS * ROWS, CELLS) for c in range(2)]
         both = jnp.concatenate(flat, axis=1)
-        spec = jnp.dot(split_cat(both, 1), fwd_ref[...], preferred_element_type=F32)
+        spec = jnp.dot(split_cat(both, 1), forward, preferred_element_type=F32)
         for h in range(2):
             re = spec[:, h * CELLS : (h + 1) * CELLS].reshape(LAYERS, ROWS, CELLS)
             im = spec[:, WAVES + h * CELLS : WAVES + (h + 1) * CELLS].reshape(LAYERS, ROWS, CELLS)
@@ -121,12 +120,11 @@
 
             def some_sources(chunk, sums):
                 sums = list(sums)
-                base = first * LAYERS + chunk * STEP
                 for s in range(STEP):
                     j = chunk * STEP + s
                     src = [spec_ref[h, j, k * ROWS : (k + 1) * ROWS] for k in range(3 * POLS)]
                     for r in range(GROUP):
-                        place = place_ref[base + (r * LAYERS + s)]
+                        place = place_ref[first + r, j]
                         for k in range(3):
                             row = pl.multiple_of(place + k * ROWS, ROWS)
                             factor = kern[h][pl.ds(row, ROWS), :]
@@ -148,15 +146,17 @@
 
         lax.fori_loop(0, LAYERS // GROUP, one_group, 0)
 
+    high, low = table_ref[2 * WAVES :, :WAVES], table_ref[2 * WAVES :, WAVES:]
+    inverse = jnp.concatenate([high, high, low], axis=0)
     for p in range(POLS):
         mixed = mixed_ref[p].reshape(LAYERS * ROWS, 2 * WAVES)
-        back = jnp.dot(split_cat(mixed, 1), inv_ref[...], preferred_element_type=F32)
+        back = jnp.dot(split_cat(mixed, 1), inverse, preferred_element_type=F32)
         for c in range(2):
             out_ref[:, 2 * p + c] = back[:, c * CELLS : (c + 1) * CELLS].reshape(LAYERS, ROWS, CELLS)
 
 
-def mix_kernel(place_ref, rows_ref, green_ref, fwd_ref, inv_ref, out_ref, spec_ref, kern_ref, mixed_ref):
-    mix_rows(rows_ref, green_ref, place_ref, fwd_ref, inv_ref, out_ref, spec_ref, kern_ref, mixed_ref)
+def mix_kernel(place_ref, rows_ref, green_ref, table_ref, out_ref, spec_ref, kern_ref, mixed_ref):
+    mix_rows(rows_ref, green_ref, place_ref, table_ref, out_ref, spec_ref, kern_ref, mixed_ref)
 
 
 def sin_pi(v):
@@ -169,7 +169,7 @@
 
 
 def adjoint_mix_kernel(
-    place_ref, first_ref, sent_ref, green_ref, fwd_ref, inv_ref,
+    place_ref, first_ref, sent_ref, green_ref, table_ref,
     out_ref, rows_ref, spec_ref, kern_ref, mixed_ref,
 ):
     sent = [sent_ref[:, :, k * CELLS : (k + 1) * CELLS] for k in range(5)]
@@ -198,7 +198,7 @@
             preferred_element_type=F32,
         )
         rows_ref[j] = (at_y[: 4 * ROWS] + at_y[4 * ROWS :]).reshape(4, ROWS, CELLS)
-    mix_rows(rows_ref, green_ref, place_ref, fwd_ref, inv_ref, out_ref, spec_ref, kern_ref, mixed_ref)
+    mix_rows(rows_ref, green_ref, place_ref, table_ref, out_ref, spec_ref, kern_ref, mixed_ref)
 
 
 def x_inverse(rows_ref, table_ref):
@@ -209,7 +209,7 @@
         for c in range(2)
     ]
     waves = jnp.concatenate(parts, axis=0)
-    cells = jnp.dot(table_ref[...], split_cat(waves, 0), preferred_element_type=F32)
+    cells = jnp.dot(thrice(table_ref[...], 1), split_cat(waves, 0), preferred_element_type=F32)
     return [
         [cells[c * CELLS : (c + 1) * CELLS, p * CELLS : (p + 1) * CELLS] for c in range(2)]
         for p in range(POLS)
@@ -273,7 +273,7 @@
 
 def sum_over_freq(copies, size):
     rings = [list(range(r, r + RING)) for r in range(0, size, RING)]
-    lines = [list(range(r, size, RING)) for r in range(RING)]
+    lines = [[r + RING * k for k in (1, 0, 2, 3)] for r in range(RING)]
     for groups in (rings, lines):
         parts = lax.all_to_all(
             copies, "freq", split_axis=0, concat_axis=0, tiled=True, axis_index_groups=groups
@@ -284,10 +284,7 @@
 
 
 def per_device(conductivity, background, green, pair_table, stations, observed, data_error, freqs):
-    x_fwd, y_fwd, y_inv, x_inv = dft_blocks()
-    x_inv = left_table(x_inv)
-    y_fwd, y_inv = right_table(y_fwd), right_table(y_inv)
-    places = (pair_table * (3 * ROWS)).reshape(-1)
+    x_fwd, y_both, x_inv = dft_blocks()
     first = (lax.axis_index("layer") * ROWS).astype(jnp.int32).reshape(1)
     rows_shape = jax.ShapeDtypeStruct((LAYERS, 4, ROWS, CELLS), F32)
     scratch = (
@@ -295,23 +292,23 @@
         pltpu.VMEM((2, KERNELS, 3 * ROWS, CELLS), F32),
         pltpu.VMEM((POLS, LAYERS, ROWS, 2 * WAVES), F32),
     )
-    rows = pl.pallas_call(
+    rows, places = pl.pallas_call(
         x_forward_kernel,
-        out_shape=rows_shape,
-        in_specs=[pl.BlockSpec(memory_space=pltpu.HBM)] * 3
-        + [pl.BlockSpec(memory_space=pl.ANY)] * 2,
-        out_specs=pl.BlockSpec(memory_space=pltpu.VMEM),
+        out_shape=[rows_shape, jax.ShapeDtypeStruct(pair_table.shape, jnp.int32)],
+        in_specs=[pl.BlockSpec(memory_space=pl.ANY)] * 5,
+        out_specs=[pl.BlockSpec(memory_space=pltpu.VMEM)] * 2,
         scratch_shapes=[
             pltpu.VMEM(conductivity.shape, F32),
             pltpu.VMEM(background.shape, F32),
             pltpu.VMEM(x_fwd.shape, BF16),
-            pltpu.SemaphoreType.DMA((3,)),
+            pltpu.VMEM(pair_table.shape, jnp.int32),
+            pltpu.SemaphoreType.DMA((4,)),
         ],
         compiler_params=pltpu.CompilerParams(vmem_limit_bytes=FIRST_BYTES),
-    )(conductivity, background, x_fwd, places, first)
+    )(conductivity, background, x_fwd, pair_table, first)
     back = call(
         mix_kernel, rows_shape, scratch, 1,
-        (places, over_layers(rows), green, y_fwd, y_inv),
+        (places, over_layers(rows), green, y_both),
     )
     total, sent = call(
         residual_kernel,
@@ -324,7 +321,7 @@
     back = call(
         adjoint_mix_kernel, rows_shape,
         (pltpu.VMEM((LAYERS, 4, ROWS, CELLS), F32),) + scratch, 2,
-        (places, first, over_layers(sent), green, y_fwd, y_inv),
+        (places, first, over_layers(sent), green, y_both),
     )
     copies = call(
         gradient_kernel,

time: 145 us -> 144 us (level)
  no operation moved by 1% of the time
where the time goes in v4:
time: 144 us
  blocking collectives  127 us (88%)
  Pallas kernels  15.8 us (11%)
    all_to_all x4, blocking collectives, over_layers(): lax.all_to_all(values, 'layer', split_axis=0, concat_axis=0, tiled=True)  105 us
    all_to_all x2, blocking collectives, sum_over_freq(): lax.all_to_all(copies, 'freq', split_axis=0, concat_axis=0, tiled=True, a...  21.7 us
    pallas_call x4, Pallas kernels, call(): pl.pallas_call(kernel, out_shape=out_shape, in_specs=specs, out_specs=out...  13.4 us

profile of v4, /device:TPU:8, one launch (start us, length us, event | category | flops | bytes accessed | tf_op | source)
XLA Modules:
  0.0 143.6 jit_solution(8835380843267290246)
XLA Ops:
  0.0 0.0 copy-start
  0.0 2.4 %shard_map.100 = (f32[32,4,8,128]{3,2,1,0:T(8,128)}, s32[32,32]{1,0:T(8,128)}) custom-call(f32[1,128,128]{2,1,0:T(8,128)} %cond_hbm.1, f32[1,2,2,1,128,128]{5,4,3,2,1,0:T(8,128)} %field_ref.1, bf16[256,512]{1,0:T(8,128)(2,1)} %constant.12.clone.table_hbm, s32[32,32]{1,0:T(8,128)} %pair_hbm.1, s32[1]{0:T(128)} %bitcast.first_any.first_ref), custom_call_target="tpu_custom_call" | custom-call | tf_op jit(solution)/shard_map/pallas_call | solution.py:295
  2.4 0.0 copy-start.1
  2.4 0.0 copy-start.4
  2.4 38.1 %all_to_all.30.rows_ref = f32[32,4,8,128]{3,2,1,0:T(8,128)S(1)} all-to-all(f32[32,4,8,128]{3,2,1,0:T(8,128)} %get-tuple-element.10), channel_id=1, replica_groups=mesh['freq'=16,'layer'=32] {'layer'}, dimensions={0} | all-to-all | bytes 1048576 | tf_op jit(solution)/shard_map/all_to_all | solution.py:271
  40.5 0.0 copy-done
  40.5 0.0 copy-done.1
  40.5 0.0 copy-done.4
  40.5 5.8 %shard_map.101 = f32[32,4,8,128]{3,2,1,0:T(8,128)S(1)} custom-call(s32[32,32]{1,0:T(8,128)S(1)} %copy-done.4, f32[32,4,8,128]{3,2,1,0:T(8,128)S(1)} %all_to_all.30.rows_ref, f32[1,2,32,8,256]{4,3,2,1,0:T(8,128)S(1)} %copy-done.1, bf16[1024,512]{1,0:T(8,128)(2,1)S(1)} %copy-done), custom_call_target="tpu_custom_call" | custom-call | tf_op jit(solution)/shard_map/pallas_call | solution.py:260
  46.3 0.0 copy-start.2
  46.3 0.0 copy-start.3
  46.3 0.0 copy-start.5
  46.3 0.0 copy-start.6
  46.3 0.0 copy-start.7
  46.4 25.5 %all_to_all.31.rows_ref = f32[32,4,8,128]{3,2,1,0:T(8,128)S(1)} all-to-all(f32[32,4,8,128]{3,2,1,0:T(8,128)S(1)} %shard_map.101), channel_id=1, replica_groups=mesh['freq'=16,'layer'=32] {'layer'}, dimensions={0} | all-to-all | bytes 1048576 | tf_op jit(solution)/shard_map/all_to_all | solution.py:271
  71.8 0.0 copy-done.2
  71.8 0.0 copy-done.3
  71.8 0.0 copy-done.5
  71.8 0.0 copy-done.6
  71.9 0.0 copy-done.7
  71.9 0.8 shard_map.102
  72.7 15.7 %all_to_all.32.sent_ref = f32[32,1,640]{2,1,0:T(1,128)S(1)} all-to-all(f32[32,1,640]{2,1,0:T(1,128)S(1)} %get-tuple-element.11), channel_id=1, replica_groups=mesh['freq'=16,'layer'=32] {'layer'}, dimensions={0} | all-to-all | bytes 163840 | tf_op jit(solution)/shard_map/all_to_all | solution.py:271
  88.4 6.4 %shard_map.103 = f32[32,4,8,128]{3,2,1,0:T(8,128)S(1)} custom-call(s32[32,32]{1,0:T(8,128)S(1)} %copy-done.4, s32[1]{0:T(128)} %bitcast.first_any.first_ref, f32[32,1,640]{2,1,0:T(1,128)S(1)} %all_to_all.32.sent_ref, f32[1,2,32,8,256]{4,3,2,1,0:T(8,128)S(1)} %copy-done.1, bf16[1024,512]{1,0:T(8,128)(2,1)S(1)} %copy-done), custom_call_target="tpu_custom_call" | custom-call | tf_op jit(solution)/shard_map/pallas_call | solution.py:260
  94.8 26.0 %all_to_all.33.rows_ref = f32[32,4,8,128]{3,2,1,0:T(8,128)S(1)} all-to-all(f32[32,4,8,128]{3,2,1,0:T(8,128)S(1)} %shard_map.103), channel_id=1, replica_groups=mesh['freq'=16,'layer'=32] {'layer'}, dimensions={0} | all-to-all | bytes 1048576 | tf_op jit(solution)/shard_map/all_to_all | solution.py:271
  120.8 0.4 shard_map.104
  121.2 10.8 %all_to_all.34 = f32[4,128,128]{2,1,0:T(8,128)S(1)} all-to-all(f32[4,128,128]{2,1,0:T(8,128)S(1)} %shard_map.104), channel_id=1, replica_groups={{0,32,64,96},{128,160,192,224},{256,288,320,352},{384,416,448,480},{1,3..., dimensions={0} | all-to-all | bytes 524288 | tf_op jit(solution)/shard_map/all_to_all | solution.py:278
  132.0 11.0 %all_to_all.35 = f32[4,128,128]{2,1,0:T(8,128)S(1)} all-to-all(f32[4,128,128]{2,1,0:T(8,128)S(1)} %broadcast_in_dim.10), channel_id=1, replica_groups={{128,0,256,384},{160,32,288,416},{192,64,320,448},{224,96,352,480},{129..., dimensions={0} | all-to-all | bytes 524288 | tf_op jit(solution)/shard_map/all_to_all | solution.py:278
  143.0 0.6 fusion
  (2 shorter events, 0.0 us)
Async XLA Ops:
  0.0 40.5 %copy-start = (bf16[1024,512]{1,0:T(8,128)(2,1)S(1)}, bf16[1024,512]{1,0:T(8,128)(2,1)}, u32[]{:S(2)}) copy-start(bf16[1024,512]{1,0:T(8,128)(2,1)} %constant.13.clone.table_ref) | copy-start | bytes 3145732
  2.4 38.2 %copy-start.1 = (f32[1,2,32,8,256]{4,3,2,1,0:T(8,128)S(1)}, f32[1,2,32,8,256]{4,3,2,1,0:T(8,128)}, u32[]{:S(2)}) copy-start(f32[1,2,32,8,256]{4,3,2,1,0:T(8,128)} %green_ref.3) | copy-start | bytes 1572868
  2.4 38.1 %copy-start.4 = (s32[32,32]{1,0:T(8,128)S(1)}, s32[32,32]{1,0:T(8,128)}, u32[]{:S(2)}) copy-start(s32[32,32]{1,0:T(8,128)} %get-tuple-element.9.place_ref) | copy-start | bytes 12292
  46.3 25.5 %copy-start.2 = (bf16[256,1024]{1,0:T(8,128)(2,1)S(1)}, bf16[256,1024]{1,0:T(8,128)(2,1)}, u32[]{:S(2)}) copy-start(bf16[256,1024]{1,0:T(8,128)(2,1)} %constant.14.clone.table_ref) | copy-start | bytes 1572868
  46.3 25.5 %copy-start.3 = (f32[1,2,2,1,128,128]{5,4,3,2,1,0:T(8,128)S(1)}, f32[1,2,2,1,128,128]{5,4,3,2,1,0:T(8,128)}, u32[]{:S(2)}) copy-start(f32[1,2,2,1,128,128]{5,4,3,2,1,0:T(8,128)} %field_ref.1) | copy-start | bytes 786436
  46.3 25.5 %copy-start.5 = (f32[1,2,2,1,128]{4,3,2,1,0:T(1,128)S(1)}, f32[1,2,2,1,128]{4,3,2,1,0:T(1,128)}, u32[]{:S(2)}) copy-start(f32[1,2,2,1,128]{4,3,2,1,0:T(1,128)} %seen_ref.1) | copy-start | bytes 6148
  46.3 25.5 %copy-start.6 = (f32[1,2,1,128]{3,2,1,0:T(1,128)S(1)}, f32[1,2,1,128]{3,2,1,0:T(1,128)}, u32[]{:S(2)}) copy-start(f32[1,2,1,128]{3,2,1,0:T(1,128)} %error_ref.1) | copy-start | bytes 3076
  46.3 25.5 %copy-start.7 = (s32[1,128]{1,0:T(1,128)S(1)}, s32[1,128]{1,0:T(1,128)}, u32[]{:S(2)}) copy-start(s32[1,128]{1,0:T(1,128)} %station_ref.1) | copy-start | bytes 1540

commit v5 on v4

--- a/solution.py
+++ b/solution.py
@@ -19,6 +19,7 @@
 GROUP = 4
 STEP = 16
 RING = 4
+SIN_PI = (0.0776576603, -0.5982912856, 2.5500775232, -5.1677100835, 3.1415926401)
 F32 = jnp.float32
 BF16 = jnp.bfloat16
 VMEM_BYTES = 40 * 1024 * 1024
@@ -94,17 +95,17 @@
 
 def mix_rows(rows_ref, green_ref, place_ref, table_ref, out_ref, spec_ref, kern_ref, mixed_ref):
     lanes = [slice(h * CELLS, (h + 1) * CELLS) for h in range(2)]
-    for h in range(2):
+    forward = thrice(table_ref[: 2 * WAVES], 0)
+    for p in range(POLS):
+        flat = [rows_ref[:, 2 * p + c].reshape(LAYERS * ROWS, CELLS) for c in range(2)]
+        both = jnp.concatenate(flat, axis=1)
+        spec = jnp.dot(split_cat(both, 1), forward, preferred_element_type=F32)
+        h = p
         g_re = green_ref[0, 0, :, :, lanes[h]]
         g_im = green_ref[0, 1, :, :, lanes[h]]
         kern_ref[h, :, 0:ROWS] = g_re + g_im
         kern_ref[h, :, ROWS : 2 * ROWS] = g_re
         kern_ref[h, :, 2 * ROWS :] = g_im
-    forward = thrice(table_ref[: 2 * WAVES], 0)
-    for p in range(POLS):
-        flat = [rows_ref[:, 2 * p + c].reshape(LAYERS * ROWS, CELLS) for c in range(2)]
-        both = jnp.concatenate(flat, axis=1)
-        spec = jnp.dot(split_cat(both, 1), forward, preferred_element_type=F32)
         for h in range(2):
             re = spec[:, h * CELLS : (h + 1) * CELLS].reshape(LAYERS, ROWS, CELLS)
             im = spec[:, WAVES + h * CELLS : WAVES + (h + 1) * CELLS].reshape(LAYERS, ROWS, CELLS)
@@ -161,10 +162,9 @@
 
 def sin_pi(v):
     square = v * v
-    total = jnp.full_like(v, math.pi**13 / math.factorial(13))
-    for order in (11, 9, 7, 5, 3, 1):
-        sign = -1.0 if (order // 2) % 2 else 1.0
-        total = total * square + sign * math.pi**order / math.factorial(order)
+    total = jnp.full_like(v, SIN_PI[0])
+    for factor in SIN_PI[1:]:
+        total = total * square + factor
     return total * v
 
 
@@ -186,10 +186,11 @@
         re, im = sent[2 * p], sent[2 * p + 1]
         rows_ref[:, 2 * p] = re * cos + im * sin
         rows_ref[:, 2 * p + 1] = im * cos - re * sin
-    y_ids = lax.broadcasted_iota(jnp.int32, (CELLS, CELLS), 0)
+    y_ids = lax.broadcasted_iota(jnp.int32, (CELLS, CELLS), 0).astype(BF16)
+    one, zero = jnp.ones((CELLS, CELLS), BF16), jnp.zeros((CELLS, CELLS), BF16)
+    y_cells = (cell & (CELLS - 1)).astype(BF16)
     for j in range(LAYERS):
-        y_cell = cell[j] & (CELLS - 1)
-        spot = jnp.where(y_ids == y_cell, 1.0, 0.0).astype(BF16)
+        spot = jnp.where(y_ids == y_cells[j], one, zero)
         values = rows_ref[j].reshape(4 * ROWS, CELLS)
         high = values.astype(BF16)
         low = (values - high.astype(F32)).astype(BF16)

time: 144 us -> 144 us (level)
  no operation moved by 1% of the time
where the time goes in v5:
time: 144 us
  blocking collectives  127 us (88%)
  Pallas kernels  15.7 us (11%)
    all_to_all x4, blocking collectives, over_layers(): lax.all_to_all(values, 'layer', split_axis=0, concat_axis=0, tiled=True)  105 us
    all_to_all x2, blocking collectives, sum_over_freq(): lax.all_to_all(copies, 'freq', split_axis=0, concat_axis=0, tiled=True, a...  21.7 us
    pallas_call x4, Pallas kernels, call(): pl.pallas_call(kernel, out_shape=out_shape, in_specs=specs, out_specs=out...  13.4 us

profile of v5, /device:TPU:8, one launch (start us, length us, event | category | flops | bytes accessed | tf_op | source)
XLA Modules:
  0.0 143.5 jit_solution(12426295667192716675)
XLA Ops:
  0.0 0.0 copy-start
  0.0 2.4 %shard_map.100 = (f32[32,4,8,128]{3,2,1,0:T(8,128)}, s32[32,32]{1,0:T(8,128)}) custom-call(f32[1,128,128]{2,1,0:T(8,128)} %cond_hbm.1, f32[1,2,2,1,128,128]{5,4,3,2,1,0:T(8,128)} %field_ref.1, bf16[256,512]{1,0:T(8,128)(2,1)} %constant.12.clone.table_hbm, s32[32,32]{1,0:T(8,128)} %pair_hbm.1, s32[1]{0:T(128)} %bitcast.first_any.first_ref), custom_call_target="tpu_custom_call" | custom-call | tf_op jit(solution)/shard_map/pallas_call | solution.py:296
  2.4 0.0 copy-start.1
  2.4 0.0 copy-start.4
  2.4 38.1 %all_to_all.30.rows_ref = f32[32,4,8,128]{3,2,1,0:T(8,128)S(1)} all-to-all(f32[32,4,8,128]{3,2,1,0:T(8,128)} %get-tuple-element.10), channel_id=1, replica_groups=mesh['freq'=16,'layer'=32] {'layer'}, dimensions={0} | all-to-all | bytes 1048576 | tf_op jit(solution)/shard_map/all_to_all | solution.py:272
  40.5 0.0 copy-done
  40.5 0.0 copy-done.1
  40.5 0.0 copy-done.4
  40.5 5.7 %shard_map.101 = f32[32,4,8,128]{3,2,1,0:T(8,128)S(1)} custom-call(s32[32,32]{1,0:T(8,128)S(1)} %copy-done.4, f32[32,4,8,128]{3,2,1,0:T(8,128)S(1)} %all_to_all.30.rows_ref, f32[1,2,32,8,256]{4,3,2,1,0:T(8,128)S(1)} %copy-done.1, bf16[1024,512]{1,0:T(8,128)(2,1)S(1)} %copy-done), custom_call_target="tpu_custom_call" | custom-call | tf_op jit(solution)/shard_map/pallas_call | solution.py:261
  46.3 0.0 copy-start.2
  46.3 0.0 copy-start.3
  46.3 0.0 copy-start.5
  46.3 0.0 copy-start.6
  46.3 0.0 copy-start.7
  46.3 25.5 %all_to_all.31.rows_ref = f32[32,4,8,128]{3,2,1,0:T(8,128)S(1)} all-to-all(f32[32,4,8,128]{3,2,1,0:T(8,128)S(1)} %shard_map.101), channel_id=1, replica_groups=mesh['freq'=16,'layer'=32] {'layer'}, dimensions={0} | all-to-all | bytes 1048576 | tf_op jit(solution)/shard_map/all_to_all | solution.py:272
  71.8 0.0 copy-done.2
  71.8 0.0 copy-done.3
  71.8 0.0 copy-done.5
  71.8 0.0 copy-done.6
  71.8 0.0 copy-done.7
  71.8 0.8 shard_map.102
  72.7 15.7 %all_to_all.32.sent_ref = f32[32,1,640]{2,1,0:T(1,128)S(1)} all-to-all(f32[32,1,640]{2,1,0:T(1,128)S(1)} %get-tuple-element.11), channel_id=1, replica_groups=mesh['freq'=16,'layer'=32] {'layer'}, dimensions={0} | all-to-all | bytes 163840 | tf_op jit(solution)/shard_map/all_to_all | solution.py:272
  88.4 6.4 %shard_map.103 = f32[32,4,8,128]{3,2,1,0:T(8,128)S(1)} custom-call(s32[32,32]{1,0:T(8,128)S(1)} %copy-done.4, s32[1]{0:T(128)} %bitcast.first_any.first_ref, f32[32,1,640]{2,1,0:T(1,128)S(1)} %all_to_all.32.sent_ref, f32[1,2,32,8,256]{4,3,2,1,0:T(8,128)S(1)} %copy-done.1, bf16[1024,512]{1,0:T(8,128)(2,1)S(1)} %copy-done), custom_call_target="tpu_custom_call" | custom-call | tf_op jit(solution)/shard_map/pallas_call | solution.py:261
  94.8 26.0 %all_to_all.33.rows_ref = f32[32,4,8,128]{3,2,1,0:T(8,128)S(1)} all-to-all(f32[32,4,8,128]{3,2,1,0:T(8,128)S(1)} %shard_map.103), channel_id=1, replica_groups=mesh['freq'=16,'layer'=32] {'layer'}, dimensions={0} | all-to-all | bytes 1048576 | tf_op jit(solution)/shard_map/all_to_all | solution.py:272
  120.7 0.4 shard_map.104
  121.1 10.8 %all_to_all.34 = f32[4,128,128]{2,1,0:T(8,128)S(1)} all-to-all(f32[4,128,128]{2,1,0:T(8,128)S(1)} %shard_map.104), channel_id=1, replica_groups={{0,32,64,96},{128,160,192,224},{256,288,320,352},{384,416,448,480},{1,3..., dimensions={0} | all-to-all | bytes 524288 | tf_op jit(solution)/shard_map/all_to_all | solution.py:279
  132.0 11.0 %all_to_all.35 = f32[4,128,128]{2,1,0:T(8,128)S(1)} all-to-all(f32[4,128,128]{2,1,0:T(8,128)S(1)} %broadcast_in_dim.10), channel_id=1, replica_groups={{128,0,256,384},{160,32,288,416},{192,64,320,448},{224,96,352,480},{129..., dimensions={0} | all-to-all | bytes 524288 | tf_op jit(solution)/shard_map/all_to_all | solution.py:279
  142.9 0.6 fusion
  (2 shorter events, 0.0 us)
Async XLA Ops:
  0.0 40.5 %copy-start = (bf16[1024,512]{1,0:T(8,128)(2,1)S(1)}, bf16[1024,512]{1,0:T(8,128)(2,1)}, u32[]{:S(2)}) copy-start(bf16[1024,512]{1,0:T(8,128)(2,1)} %constant.13.clone.table_ref) | copy-start | bytes 3145732
  2.4 38.2 %copy-start.1 = (f32[1,2,32,8,256]{4,3,2,1,0:T(8,128)S(1)}, f32[1,2,32,8,256]{4,3,2,1,0:T(8,128)}, u32[]{:S(2)}) copy-start(f32[1,2,32,8,256]{4,3,2,1,0:T(8,128)} %green_ref.3) | copy-start | bytes 1572868
  2.4 38.1 %copy-start.4 = (s32[32,32]{1,0:T(8,128)S(1)}, s32[32,32]{1,0:T(8,128)}, u32[]{:S(2)}) copy-start(s32[32,32]{1,0:T(8,128)} %get-tuple-element.9.place_ref) | copy-start | bytes 12292
  46.3 25.5 %copy-start.2 = (bf16[256,1024]{1,0:T(8,128)(2,1)S(1)}, bf16[256,1024]{1,0:T(8,128)(2,1)}, u32[]{:S(2)}) copy-start(bf16[256,1024]{1,0:T(8,128)(2,1)} %constant.14.clone.table_ref) | copy-start | bytes 1572868
  46.3 25.5 %copy-start.3 = (f32[1,2,2,1,128,128]{5,4,3,2,1,0:T(8,128)S(1)}, f32[1,2,2,1,128,128]{5,4,3,2,1,0:T(8,128)}, u32[]{:S(2)}) copy-start(f32[1,2,2,1,128,128]{5,4,3,2,1,0:T(8,128)} %field_ref.1) | copy-start | bytes 786436
  46.3 25.5 %copy-start.5 = (f32[1,2,2,1,128]{4,3,2,1,0:T(1,128)S(1)}, f32[1,2,2,1,128]{4,3,2,1,0:T(1,128)}, u32[]{:S(2)}) copy-start(f32[1,2,2,1,128]{4,3,2,1,0:T(1,128)} %seen_ref.1) | copy-start | bytes 6148
  46.3 25.5 %copy-start.6 = (f32[1,2,1,128]{3,2,1,0:T(1,128)S(1)}, f32[1,2,1,128]{3,2,1,0:T(1,128)}, u32[]{:S(2)}) copy-start(f32[1,2,1,128]{3,2,1,0:T(1,128)} %error_ref.1) | copy-start | bytes 3076
  46.3 25.5 %copy-start.7 = (s32[1,128]{1,0:T(1,128)S(1)}, s32[1,128]{1,0:T(1,128)}, u32[]{:S(2)}) copy-start(s32[1,128]{1,0:T(1,128)} %station_ref.1) | copy-start | bytes 1540

commit v6 on v5

--- a/solution.py
+++ b/solution.py
@@ -59,10 +59,9 @@
 
 
 def x_forward_kernel(
-    cond_hbm, field_hbm, table_hbm, pair_hbm, first_any,
+    cond_hbm, field_hbm, table_hbm, pair_hbm,
     out_ref, place_ref, cond_ref, field_ref, table_ref, pair_ref, sems,
 ):
-    del first_any
     moves = ((field_hbm, field_ref), (cond_hbm, cond_ref), (table_hbm, table_ref), (pair_hbm, pair_ref))
     copies = [
         pltpu.make_async_copy(source, target, sems.at[n])
@@ -93,7 +92,7 @@
             out_ref[:, 2 * p + c] = rows[:, at : at + CELLS].reshape(LAYERS, ROWS, CELLS)
 
 
-def mix_rows(rows_ref, green_ref, place_ref, table_ref, out_ref, spec_ref, kern_ref, mixed_ref):
+def mix_rows(rows_ref, green_ref, place_ref, places, table_ref, out_ref, spec_ref, kern_ref, mixed_ref):
     lanes = [slice(h * CELLS, (h + 1) * CELLS) for h in range(2)]
     forward = thrice(table_ref[: 2 * WAVES], 0)
     for p in range(POLS):
@@ -113,6 +112,7 @@
                 at = (3 * p + k) * ROWS
                 spec_ref[h, :, at : at + ROWS] = value
 
+    places.wait()
     kern = [kern_ref.at[h].reshape(KERNELS * 3 * ROWS, CELLS) for h in range(2)]
     for h in range(2):
 
@@ -156,8 +156,12 @@
             out_ref[:, 2 * p + c] = back[:, c * CELLS : (c + 1) * CELLS].reshape(LAYERS, ROWS, CELLS)
 
 
-def mix_kernel(place_ref, rows_ref, green_ref, table_ref, out_ref, spec_ref, kern_ref, mixed_ref):
-    mix_rows(rows_ref, green_ref, place_ref, table_ref, out_ref, spec_ref, kern_ref, mixed_ref)
+def mix_kernel(
+    place_any, rows_ref, green_ref, table_ref, out_ref, spec_ref, kern_ref, mixed_ref, place_ref, sem
+):
+    places = pltpu.make_async_copy(place_any, place_ref, sem)
+    places.start()
+    mix_rows(rows_ref, green_ref, place_ref, places, table_ref, out_ref, spec_ref, kern_ref, mixed_ref)
 
 
 def sin_pi(v):
@@ -169,13 +173,15 @@
 
 
 def adjoint_mix_kernel(
-    place_ref, first_ref, sent_ref, green_ref, table_ref,
-    out_ref, rows_ref, spec_ref, kern_ref, mixed_ref,
+    place_any, sent_ref, green_ref, table_ref,
+    out_ref, rows_ref, spec_ref, kern_ref, mixed_ref, place_ref, sem,
 ):
+    places = pltpu.make_async_copy(place_any, place_ref, sem)
+    places.start()
     sent = [sent_ref[:, :, k * CELLS : (k + 1) * CELLS] for k in range(5)]
     cell = sent[4].astype(jnp.int32)
     x_cell = cell >> 7
-    wave = first_ref[0] + lax.broadcasted_iota(jnp.int32, (LAYERS, ROWS, CELLS), 1)
+    wave = lax.axis_index("layer") * ROWS + lax.broadcasted_iota(jnp.int32, (LAYERS, ROWS, CELLS), 1)
     turn = (wave * x_cell) & (WAVES - 1)
     u = (turn.astype(F32) - WAVES / 2) * (2.0 / WAVES)
     size = jnp.abs(u)
@@ -199,7 +205,7 @@
             preferred_element_type=F32,
         )
         rows_ref[j] = (at_y[: 4 * ROWS] + at_y[4 * ROWS :]).reshape(4, ROWS, CELLS)
-    mix_rows(rows_ref, green_ref, place_ref, table_ref, out_ref, spec_ref, kern_ref, mixed_ref)
+    mix_rows(rows_ref, green_ref, place_ref, places, table_ref, out_ref, spec_ref, kern_ref, mixed_ref)
 
 
 def x_inverse(rows_ref, table_ref):
@@ -251,9 +257,9 @@
     out_ref[...] = jnp.broadcast_to(term[None], (RING, CELLS, CELLS))
 
 
-def call(kernel, out_shape, scratch=(), smem=0, operands=()):
-    specs = [pl.BlockSpec(memory_space=pltpu.SMEM)] * smem
-    specs += [pl.BlockSpec(memory_space=pltpu.VMEM)] * (len(operands) - smem)
+def call(kernel, out_shape, scratch=(), loose=0, operands=()):
+    specs = [pl.BlockSpec(memory_space=pl.ANY)] * loose
+    specs += [pl.BlockSpec(memory_space=pltpu.VMEM)] * (len(operands) - loose)
     if isinstance(out_shape, list):
         out_specs = [pl.BlockSpec(memory_space=pltpu.VMEM)] * len(out_shape)
     else:
@@ -286,17 +292,18 @@
 
 def per_device(conductivity, background, green, pair_table, stations, observed, data_error, freqs):
     x_fwd, y_both, x_inv = dft_blocks()
-    first = (lax.axis_index("layer") * ROWS).astype(jnp.int32).reshape(1)
     rows_shape = jax.ShapeDtypeStruct((LAYERS, 4, ROWS, CELLS), F32)
     scratch = (
         pltpu.VMEM((2, LAYERS, 3 * POLS * ROWS, CELLS), F32),
         pltpu.VMEM((2, KERNELS, 3 * ROWS, CELLS), F32),
         pltpu.VMEM((POLS, LAYERS, ROWS, 2 * WAVES), F32),
+        pltpu.SMEM(pair_table.shape, jnp.int32),
+        pltpu.SemaphoreType.DMA(()),
     )
     rows, places = pl.pallas_call(
         x_forward_kernel,
         out_shape=[rows_shape, jax.ShapeDtypeStruct(pair_table.shape, jnp.int32)],
-        in_specs=[pl.BlockSpec(memory_space=pl.ANY)] * 5,
+        in_specs=[pl.BlockSpec(memory_space=pl.ANY)] * 4,
         out_specs=[pl.BlockSpec(memory_space=pltpu.VMEM)] * 2,
         scratch_shapes=[
             pltpu.VMEM(conductivity.shape, F32),
@@ -306,7 +313,7 @@
             pltpu.SemaphoreType.DMA((4,)),
         ],
         compiler_params=pltpu.CompilerParams(vmem_limit_bytes=FIRST_BYTES),
-    )(conductivity, background, x_fwd, pair_table, first)
+    )(conductivity, background, x_fwd, pair_table)
     back = call(
         mix_kernel, rows_shape, scratch, 1,
         (places, over_layers(rows), green, y_both),
@@ -321,8 +328,8 @@
     )
     back = call(
         adjoint_mix_kernel, rows_shape,
-        (pltpu.VMEM((LAYERS, 4, ROWS, CELLS), F32),) + scratch, 2,
-        (places, first, over_layers(sent), green, y_both),
+        (pltpu.VMEM((LAYERS, 4, ROWS, CELLS), F32),) + scratch, 1,
+        (places, over_layers(sent), green, y_both),
     )
     copies = call(
         gradient_kernel,

time: 144 us -> 143 us (level)
  no operation moved by 1% of the time
where the time goes in v6:
time: 143 us; the launch traced here: 142 us
  blocking collectives  127 us (89%)
  Pallas kernels  14.4 us (10%)
    all_to_all x4, blocking collectives, over_layers(): lax.all_to_all(values, 'layer', split_axis=0, concat_axis=0, tiled=True)  105 us
    all_to_all x2, blocking collectives, sum_over_freq(): lax.all_to_all(copies, 'freq', split_axis=0, concat_axis=0, tiled=True, a...  21.7 us
    pallas_call x4, Pallas kernels, call(): pl.pallas_call(kernel, out_shape=out_shape, in_specs=specs, out_specs=out...  12 us

profile of v6, /device:TPU:8, one launch (start us, length us, event | category | flops | bytes accessed | tf_op | source)
XLA Modules:
  0.0 142.2 jit_solution(7710363396816252924)
XLA Ops:
  0.0 0.0 copy-start
  0.0 2.4 %shard_map.100 = (f32[32,4,8,128]{3,2,1,0:T(8,128)}, s32[32,32]{1,0:T(8,128)}) custom-call(f32[1,128,128]{2,1,0:T(8,128)} %cond_hbm.1, f32[1,2,2,1,128,128]{5,4,3,2,1,0:T(8,128)} %field_ref.1, bf16[256,512]{1,0:T(8,128)(2,1)} %constant.6.clone.table_hbm, s32[32,32]{1,0:T(8,128)} %pair_hbm.1), custom_call_target="tpu_custom_call" | custom-call | tf_op jit(solution)/shard_map/pallas_call | solution.py:303
  2.4 0.0 copy-start.2
  2.4 0.0 copy-start.4
  2.4 38.1 %all_to_all.30.rows_ref = f32[32,4,8,128]{3,2,1,0:T(8,128)S(1)} all-to-all(f32[32,4,8,128]{3,2,1,0:T(8,128)} %get-tuple-element.10), channel_id=1, replica_groups=mesh['freq'=16,'layer'=32] {'layer'}, dimensions={0} | all-to-all | bytes 1048576 | tf_op jit(solution)/shard_map/all_to_all | solution.py:278
  40.5 0.0 copy-done
  40.5 0.0 copy-done.2
  40.5 0.0 copy-done.4
  40.5 5.2 %shard_map.101 = f32[32,4,8,128]{3,2,1,0:T(8,128)S(1)} custom-call(s32[32,32]{1,0:T(8,128)S(1)} %copy-done.4, f32[32,4,8,128]{3,2,1,0:T(8,128)S(1)} %all_to_all.30.rows_ref, f32[1,2,32,8,256]{4,3,2,1,0:T(8,128)S(1)} %copy-done.2, bf16[1024,512]{1,0:T(8,128)(2,1)S(1)} %copy-done), custom_call_target="tpu_custom_call" | custom-call | tf_op jit(solution)/shard_map/pallas_call | solution.py:267
  45.7 0.0 copy-start.1
  45.7 0.0 copy-start.3
  45.7 0.0 copy-start.5
  45.7 0.0 copy-start.6
  45.8 0.0 copy-start.7
  45.8 25.5 %all_to_all.31.rows_ref = f32[32,4,8,128]{3,2,1,0:T(8,128)S(1)} all-to-all(f32[32,4,8,128]{3,2,1,0:T(8,128)S(1)} %shard_map.101), channel_id=1, replica_groups=mesh['freq'=16,'layer'=32] {'layer'}, dimensions={0} | all-to-all | bytes 1048576 | tf_op jit(solution)/shard_map/all_to_all | solution.py:278
  71.3 0.0 copy-done.1
  71.3 0.0 copy-done.3
  71.3 0.0 copy-done.5
  71.3 0.0 copy-done.6
  71.3 0.0 copy-done.7
  71.3 0.8 shard_map.102
  72.1 15.7 %all_to_all.32.sent_ref = f32[32,1,640]{2,1,0:T(1,128)S(1)} all-to-all(f32[32,1,640]{2,1,0:T(1,128)S(1)} %get-tuple-element.11), channel_id=1, replica_groups=mesh['freq'=16,'layer'=32] {'layer'}, dimensions={0} | all-to-all | bytes 163840 | tf_op jit(solution)/shard_map/all_to_all | solution.py:278
  87.8 5.7 %shard_map.103 = f32[32,4,8,128]{3,2,1,0:T(8,128)S(1)} custom-call(s32[32,32]{1,0:T(8,128)S(1)} %copy-done.4, f32[32,1,640]{2,1,0:T(1,128)S(1)} %all_to_all.32.sent_ref, f32[1,2,32,8,256]{4,3,2,1,0:T(8,128)S(1)} %copy-done.2, bf16[1024,512]{1,0:T(8,128)(2,1)S(1)} %copy-done), custom_call_target="tpu_custom_call" | custom-call | tf_op jit(solution)/shard_map/pallas_call | solution.py:267
  93.5 26.0 %all_to_all.33.rows_ref = f32[32,4,8,128]{3,2,1,0:T(8,128)S(1)} all-to-all(f32[32,4,8,128]{3,2,1,0:T(8,128)S(1)} %shard_map.103), channel_id=1, replica_groups=mesh['freq'=16,'layer'=32] {'layer'}, dimensions={0} | all-to-all | bytes 1048576 | tf_op jit(solution)/shard_map/all_to_all | solution.py:278
  119.4 0.4 shard_map.104
  119.8 10.8 %all_to_all.34 = f32[4,128,128]{2,1,0:T(8,128)S(1)} all-to-all(f32[4,128,128]{2,1,0:T(8,128)S(1)} %shard_map.104), channel_id=1, replica_groups={{0,32,64,96},{128,160,192,224},{256,288,320,352},{384,416,448,480},{1,3..., dimensions={0} | all-to-all | bytes 524288 | tf_op jit(solution)/shard_map/all_to_all | solution.py:285
  130.6 11.0 %all_to_all.35 = f32[4,128,128]{2,1,0:T(8,128)S(1)} all-to-all(f32[4,128,128]{2,1,0:T(8,128)S(1)} %broadcast_in_dim.10), channel_id=1, replica_groups={{128,0,256,384},{160,32,288,416},{192,64,320,448},{224,96,352,480},{129..., dimensions={0} | all-to-all | bytes 524288 | tf_op jit(solution)/shard_map/all_to_all | solution.py:285
  141.6 0.6 fusion
  (2 shorter events, 0.0 us)
Async XLA Ops:
  0.0 40.5 %copy-start = (bf16[1024,512]{1,0:T(8,128)(2,1)S(1)}, bf16[1024,512]{1,0:T(8,128)(2,1)}, u32[]{:S(2)}) copy-start(bf16[1024,512]{1,0:T(8,128)(2,1)} %constant.7.clone.table_ref) | copy-start | bytes 3145732
  2.4 38.2 %copy-start.2 = (f32[1,2,32,8,256]{4,3,2,1,0:T(8,128)S(1)}, f32[1,2,32,8,256]{4,3,2,1,0:T(8,128)}, u32[]{:S(2)}) copy-start(f32[1,2,32,8,256]{4,3,2,1,0:T(8,128)} %green_ref.3) | copy-start | bytes 1572868
  2.4 38.1 %copy-start.4 = (s32[32,32]{1,0:T(8,128)S(1)}, s32[32,32]{1,0:T(8,128)}, u32[]{:S(2)}) copy-start(s32[32,32]{1,0:T(8,128)} %get-tuple-element.9.place_any) | copy-start | bytes 12292
  45.7 25.5 %copy-start.1 = (bf16[256,1024]{1,0:T(8,128)(2,1)S(1)}, bf16[256,1024]{1,0:T(8,128)(2,1)}, u32[]{:S(2)}) copy-start(bf16[256,1024]{1,0:T(8,128)(2,1)} %constant.8.clone.table_ref) | copy-start | bytes 1572868
  45.7 25.5 %copy-start.3 = (f32[1,2,2,1,128,128]{5,4,3,2,1,0:T(8,128)S(1)}, f32[1,2,2,1,128,128]{5,4,3,2,1,0:T(8,128)}, u32[]{:S(2)}) copy-start(f32[1,2,2,1,128,128]{5,4,3,2,1,0:T(8,128)} %field_ref.1) | copy-start | bytes 786436
  45.7 25.5 %copy-start.5 = (f32[1,2,2,1,128]{4,3,2,1,0:T(1,128)S(1)}, f32[1,2,2,1,128]{4,3,2,1,0:T(1,128)}, u32[]{:S(2)}) copy-start(f32[1,2,2,1,128]{4,3,2,1,0:T(1,128)} %seen_ref.1) | copy-start | bytes 6148
  45.7 25.5 %copy-start.6 = (f32[1,2,1,128]{3,2,1,0:T(1,128)S(1)}, f32[1,2,1,128]{3,2,1,0:T(1,128)}, u32[]{:S(2)}) copy-start(f32[1,2,1,128]{3,2,1,0:T(1,128)} %error_ref.1) | copy-start | bytes 3076
  45.8 25.5 %copy-start.7 = (s32[1,128]{1,0:T(1,128)S(1)}, s32[1,128]{1,0:T(1,128)}, u32[]{:S(2)}) copy-start(s32[1,128]{1,0:T(1,128)} %station_ref.1) | copy-start | bytes 1540

commit v7 on v6

--- a/solution.py
+++ b/solution.py
@@ -19,6 +19,7 @@
 GROUP = 4
 STEP = 16
 RING = 4
+LEAD = 24
 SIN_PI = (0.0776576603, -0.5982912856, 2.5500775232, -5.1677100835, 3.1415926401)
 F32 = jnp.float32
 BF16 = jnp.bfloat16
@@ -37,10 +38,11 @@
     cells = np.arange(CELLS)[None, :]
     angles = (waves * cells % WAVES) * (2.0 * math.pi / WAVES)
     cos, sin = np.cos(angles), np.sin(angles)
-    x_fwd = np.concatenate([cos, sin], axis=1)
+    parts = np.arange(WAVES).reshape(LAYERS, ROWS)[np.arange(LAYERS) ^ LEAD].reshape(-1)
+    x_fwd = np.concatenate([cos, sin], axis=1)[parts]
     y_fwd = np.block([[cos.T, -sin.T], [sin.T, cos.T]])
     y_inv = np.block([[cos, sin], [-sin, cos]]) / WAVES
-    x_inv = np.block([[cos.T, -sin.T], [sin.T, cos.T]]) / WAVES
+    x_inv = np.block([[cos[parts].T, -sin[parts].T], [sin[parts].T, cos[parts].T]]) / WAVES
     y_both = np.concatenate(
         [np.concatenate(halves(y_fwd), axis=0), np.concatenate(halves(y_inv), axis=1)], axis=0
     )
@@ -118,14 +120,16 @@
 
         def one_group(group, carry, h=h):
             first = group * GROUP
+            first_layer = (group ^ (LEAD // GROUP)) * GROUP
 
             def some_sources(chunk, sums):
                 sums = list(sums)
                 for s in range(STEP):
                     j = chunk * STEP + s
                     src = [spec_ref[h, j, k * ROWS : (k + 1) * ROWS] for k in range(3 * POLS)]
+                    layer = (chunk ^ (LEAD // STEP)) * STEP + (s ^ (LEAD % STEP))
                     for r in range(GROUP):
-                        place = place_ref[first + r, j]
+                        place = place_ref[first_layer + r, layer]
                         for k in range(3):
                             row = pl.multiple_of(place + k * ROWS, ROWS)
                             factor = kern[h][pl.ds(row, ROWS), :]
@@ -275,12 +279,15 @@
 
 
 def over_layers(values):
-    return lax.all_to_all(values, "layer", split_axis=0, concat_axis=0, tiled=True)
+    groups = [[k ^ LEAD for k in range(LAYERS)]]
+    return lax.all_to_all(
+        values, "layer", split_axis=0, concat_axis=0, tiled=True, axis_index_groups=groups
+    )
 
 
 def sum_over_freq(copies, size):
     rings = [list(range(r, r + RING)) for r in range(0, size, RING)]
-    lines = [[r + RING * k for k in (1, 0, 2, 3)] for r in range(RING)]
+    lines = [[r + RING * k for k in (2, 1, 0, 3)] for r in range(RING)]
     for groups in (rings, lines):
         parts = lax.all_to_all(
             copies, "freq", split_axis=0, concat_axis=0, tiled=True, axis_index_groups=groups

time: 143 us -> 135 us (0.944)
  blocking collectives: 127 us -> 119 us
    all_to_all x4, blocking collectives: 105 us -> 98 us  [over_layers(): lax.all_to_all(values, 'layer', split_axis=0, concat_axis=0, tiled=True,...]
where the time goes in v7:
time: 135 us
  blocking collectives  119 us (88%)
  Pallas kernels  14.5 us (11%)
    all_to_all x4, blocking collectives, over_layers(): lax.all_to_all(values, 'layer', split_axis=0, concat_axis=0, tiled=True,...  98 us
    all_to_all x2, blocking collectives, sum_over_freq(): lax.all_to_all(copies, 'freq', split_axis=0, concat_axis=0, tiled=True, a...  21.3 us
    pallas_call x4, Pallas kernels, call(): pl.pallas_call(kernel, out_shape=out_shape, in_specs=specs, out_specs=out...  12.1 us

profile of v7, /device:TPU:8, one launch (start us, length us, event | category | flops | bytes accessed | tf_op | source)
XLA Modules:
  0.0 134.6 jit_solution(3209659274427316788)
XLA Ops:
  0.0 0.0 copy-start
  0.0 2.4 %shard_map.100 = (f32[32,4,8,128]{3,2,1,0:T(8,128)}, s32[32,32]{1,0:T(8,128)}) custom-call(f32[1,128,128]{2,1,0:T(8,128)} %cond_hbm.1, f32[1,2,2,1,128,128]{5,4,3,2,1,0:T(8,128)} %field_ref.1, bf16[256,512]{1,0:T(8,128)(2,1)} %constant.6.clone.table_hbm, s32[32,32]{1,0:T(8,128)} %pair_hbm.1), custom_call_target="tpu_custom_call" | custom-call | tf_op jit(solution)/shard_map/pallas_call | solution.py:310
  2.4 0.0 copy-start.2
  2.4 0.0 copy-start.4
  2.4 30.8 %all_to_all.30.rows_ref = f32[32,4,8,128]{3,2,1,0:T(8,128)S(1)} all-to-all(f32[32,4,8,128]{3,2,1,0:T(8,128)} %get-tuple-element.10), channel_id=1, replica_groups={{24,25,26,27,28,29,30,31,16,17,18,19,20,21,22,23,8,9,10,11,12,13,14,15,..., dimensions={0} | all-to-all | bytes 1048576 | tf_op jit(solution)/shard_map/all_to_all | solution.py:283
  33.2 0.0 copy-done
  33.2 0.0 copy-done.2
  33.2 0.0 copy-done.4
  33.2 5.2 %shard_map.101 = f32[32,4,8,128]{3,2,1,0:T(8,128)S(1)} custom-call(s32[32,32]{1,0:T(8,128)S(1)} %copy-done.4, f32[32,4,8,128]{3,2,1,0:T(8,128)S(1)} %all_to_all.30.rows_ref, f32[1,2,32,8,256]{4,3,2,1,0:T(8,128)S(1)} %copy-done.2, bf16[1024,512]{1,0:T(8,128)(2,1)S(1)} %copy-done), custom_call_target="tpu_custom_call" | custom-call | tf_op jit(solution)/shard_map/pallas_call | solution.py:271
  38.5 0.0 copy-start.1
  38.5 0.0 copy-start.3
  38.5 0.0 copy-start.5
  38.5 0.0 copy-start.6
  38.5 0.0 copy-start.7
  38.5 25.5 %all_to_all.31.rows_ref = f32[32,4,8,128]{3,2,1,0:T(8,128)S(1)} all-to-all(f32[32,4,8,128]{3,2,1,0:T(8,128)S(1)} %shard_map.101), channel_id=1, replica_groups={{24,25,26,27,28,29,30,31,16,17,18,19,20,21,22,23,8,9,10,11,12,13,14,15,..., dimensions={0} | all-to-all | bytes 1048576 | tf_op jit(solution)/shard_map/all_to_all | solution.py:283
  64.0 0.0 copy-done.1
  64.0 0.0 copy-done.3
  64.0 0.0 copy-done.5
  64.0 0.0 copy-done.6
  64.0 0.0 copy-done.7
  64.1 0.8 shard_map.102
  64.9 15.7 %all_to_all.32.sent_ref = f32[32,1,640]{2,1,0:T(1,128)S(1)} all-to-all(f32[32,1,640]{2,1,0:T(1,128)S(1)} %get-tuple-element.11), channel_id=1, replica_groups={{24,25,26,27,28,29,30,31,16,17,18,19,20,21,22,23,8,9,10,11,12,13,14,15,..., dimensions={0} | all-to-all | bytes 163840 | tf_op jit(solution)/shard_map/all_to_all | solution.py:283
  80.5 5.7 %shard_map.103 = f32[32,4,8,128]{3,2,1,0:T(8,128)S(1)} custom-call(s32[32,32]{1,0:T(8,128)S(1)} %copy-done.4, f32[32,1,640]{2,1,0:T(1,128)S(1)} %all_to_all.32.sent_ref, f32[1,2,32,8,256]{4,3,2,1,0:T(8,128)S(1)} %copy-done.2, bf16[1024,512]{1,0:T(8,128)(2,1)S(1)} %copy-done), custom_call_target="tpu_custom_call" | custom-call | tf_op jit(solution)/shard_map/pallas_call | solution.py:271
  86.2 26.0 %all_to_all.33.rows_ref = f32[32,4,8,128]{3,2,1,0:T(8,128)S(1)} all-to-all(f32[32,4,8,128]{3,2,1,0:T(8,128)S(1)} %shard_map.103), channel_id=1, replica_groups={{24,25,26,27,28,29,30,31,16,17,18,19,20,21,22,23,8,9,10,11,12,13,14,15,..., dimensions={0} | all-to-all | bytes 1048576 | tf_op jit(solution)/shard_map/all_to_all | solution.py:283
  112.2 0.4 shard_map.104
  112.6 11.0 %all_to_all.34 = f32[4,128,128]{2,1,0:T(8,128)S(1)} all-to-all(f32[4,128,128]{2,1,0:T(8,128)S(1)} %shard_map.104), channel_id=1, replica_groups={{0,32,64,96},{128,160,192,224},{256,288,320,352},{384,416,448,480},{1,3..., dimensions={0} | all-to-all | bytes 524288 | tf_op jit(solution)/shard_map/all_to_all | solution.py:292
  123.7 10.2 %all_to_all.35 = f32[4,128,128]{2,1,0:T(8,128)S(1)} all-to-all(f32[4,128,128]{2,1,0:T(8,128)S(1)} %broadcast_in_dim.10), channel_id=1, replica_groups={{256,128,0,384},{288,160,32,416},{320,192,64,448},{352,224,96,480},{257..., dimensions={0} | all-to-all | bytes 524288 | tf_op jit(solution)/shard_map/all_to_all | solution.py:292
  134.0 0.6 fusion
  (2 shorter events, 0.0 us)
Async XLA Ops:
  0.0 33.2 %copy-start = (bf16[1024,512]{1,0:T(8,128)(2,1)S(1)}, bf16[1024,512]{1,0:T(8,128)(2,1)}, u32[]{:S(2)}) copy-start(bf16[1024,512]{1,0:T(8,128)(2,1)} %constant.7.clone.table_ref) | copy-start | bytes 3145732
  2.4 30.9 %copy-start.2 = (f32[1,2,32,8,256]{4,3,2,1,0:T(8,128)S(1)}, f32[1,2,32,8,256]{4,3,2,1,0:T(8,128)}, u32[]{:S(2)}) copy-start(f32[1,2,32,8,256]{4,3,2,1,0:T(8,128)} %green_ref.3) | copy-start | bytes 1572868
  2.4 30.9 %copy-start.4 = (s32[32,32]{1,0:T(8,128)S(1)}, s32[32,32]{1,0:T(8,128)}, u32[]{:S(2)}) copy-start(s32[32,32]{1,0:T(8,128)} %get-tuple-element.9.place_any) | copy-start | bytes 12292
  38.5 25.6 %copy-start.1 = (bf16[256,1024]{1,0:T(8,128)(2,1)S(1)}, bf16[256,1024]{1,0:T(8,128)(2,1)}, u32[]{:S(2)}) copy-start(bf16[256,1024]{1,0:T(8,128)(2,1)} %constant.8.clone.table_ref) | copy-start | bytes 1572868
  38.5 25.5 %copy-start.3 = (f32[1,2,2,1,128,128]{5,4,3,2,1,0:T(8,128)S(1)}, f32[1,2,2,1,128,128]{5,4,3,2,1,0:T(8,128)}, u32[]{:S(2)}) copy-start(f32[1,2,2,1,128,128]{5,4,3,2,1,0:T(8,128)} %field_ref.1) | copy-start | bytes 786436
  38.5 25.5 %copy-start.5 = (f32[1,2,2,1,128]{4,3,2,1,0:T(1,128)S(1)}, f32[1,2,2,1,128]{4,3,2,1,0:T(1,128)}, u32[]{:S(2)}) copy-start(f32[1,2,2,1,128]{4,3,2,1,0:T(1,128)} %seen_ref.1) | copy-start | bytes 6148
  38.5 25.5 %copy-start.6 = (f32[1,2,1,128]{3,2,1,0:T(1,128)S(1)}, f32[1,2,1,128]{3,2,1,0:T(1,128)}, u32[]{:S(2)}) copy-start(f32[1,2,1,128]{3,2,1,0:T(1,128)} %error_ref.1) | copy-start | bytes 3076
  38.5 25.5 %copy-start.7 = (s32[1,128]{1,0:T(1,128)S(1)}, s32[1,128]{1,0:T(1,128)}, u32[]{:S(2)}) copy-start(s32[1,128]{1,0:T(1,128)} %station_ref.1) | copy-start | bytes 1540

commit v8 on v7

--- a/solution.py
+++ b/solution.py
@@ -19,7 +19,7 @@
 GROUP = 4
 STEP = 16
 RING = 4
-LEAD = 24
+LEAD = 27
 SIN_PI = (0.0776576603, -0.5982912856, 2.5500775232, -5.1677100835, 3.1415926401)
 F32 = jnp.float32
 BF16 = jnp.bfloat16
@@ -129,7 +129,7 @@
                     src = [spec_ref[h, j, k * ROWS : (k + 1) * ROWS] for k in range(3 * POLS)]
                     layer = (chunk ^ (LEAD // STEP)) * STEP + (s ^ (LEAD % STEP))
                     for r in range(GROUP):
-                        place = place_ref[first_layer + r, layer]
+                        place = place_ref[first_layer + (r ^ (LEAD % GROUP)), layer]
                         for k in range(3):
                             row = pl.multiple_of(place + k * ROWS, ROWS)
                             factor = kern[h][pl.ds(row, ROWS), :]
@@ -286,11 +286,16 @@
 
 
 def sum_over_freq(copies, size):
-    rings = [list(range(r, r + RING)) for r in range(0, size, RING)]
+    rings = [[r + k for k in (2, 1, 0, 3)] for r in range(0, size, RING)]
     lines = [[r + RING * k for k in (2, 1, 0, 3)] for r in range(RING)]
-    for groups in (rings, lines):
+    for by_core in ((rings, lines), (lines, rings)):
+        groups = [
+            [member * LAYERS + layer for member in group]
+            for layer in range(LAYERS)
+            for group in by_core[layer % 2]
+        ]
         parts = lax.all_to_all(
-            copies, "freq", split_axis=0, concat_axis=0, tiled=True, axis_index_groups=groups
+            copies, ("freq", "layer"), split_axis=0, concat_axis=0, tiled=True, axis_index_groups=groups
         )
         total = (parts[0] + parts[1]) + (parts[2] + parts[3])
         copies = jnp.broadcast_to(total[None], copies.shape)

time: 135 us -> 129 us (0.956)
  the two profiles are of different devices: /device:TPU:8 before, /device:TPU:60 now
where the time goes in v8:
time: 129 us
  blocking collectives  113 us (88%)
  Pallas kernels  14.5 us (11%)
    all_to_all x4, blocking collectives, over_layers(): lax.all_to_all(values, 'layer', split_axis=0, concat_axis=0, tiled=True,...  94.8 us
    all_to_all x2, blocking collectives, sum_over_freq(): lax.all_to_all(copies, ('freq', 'layer'), split_axis=0, concat_axis=0, ti...  18.7 us
    pallas_call x4, Pallas kernels, call(): pl.pallas_call(kernel, out_shape=out_shape, in_specs=specs, out_specs=out...  12.2 us

profile of v8, /device:TPU:60, one launch (start us, length us, event | category | flops | bytes accessed | tf_op | source)
XLA Modules:
  0.0 128.9 jit_solution(5045409801011607386)
XLA Ops:
  0.0 0.0 copy-start
  0.0 2.4 %shard_map.100 = (f32[32,4,8,128]{3,2,1,0:T(8,128)}, s32[32,32]{1,0:T(8,128)}) custom-call(f32[1,128,128]{2,1,0:T(8,128)} %cond_hbm.1, f32[1,2,2,1,128,128]{5,4,3,2,1,0:T(8,128)} %field_ref.1, bf16[256,512]{1,0:T(8,128)(2,1)} %constant.6.clone.table_hbm, s32[32,32]{1,0:T(8,128)} %pair_hbm.1), custom_call_target="tpu_custom_call" | custom-call | tf_op jit(solution)/shard_map/pallas_call | solution.py:315
  2.4 0.0 copy-start.2
  2.4 0.0 copy-start.4
  2.4 29.8 %all_to_all.30.rows_ref = f32[32,4,8,128]{3,2,1,0:T(8,128)S(1)} all-to-all(f32[32,4,8,128]{3,2,1,0:T(8,128)} %get-tuple-element.10), channel_id=1, replica_groups={{27,26,25,24,31,30,29,28,19,18,17,16,23,22,21,20,11,10,9,8,15,14,13,12,..., dimensions={0} | all-to-all | bytes 1048576 | tf_op jit(solution)/shard_map/all_to_all | solution.py:283
  32.2 0.0 copy-done
  32.2 0.0 copy-done.2
  32.2 0.0 copy-done.4
  32.2 5.2 %shard_map.101 = f32[32,4,8,128]{3,2,1,0:T(8,128)S(1)} custom-call(s32[32,32]{1,0:T(8,128)S(1)} %copy-done.4, f32[32,4,8,128]{3,2,1,0:T(8,128)S(1)} %all_to_all.30.rows_ref, f32[1,2,32,8,256]{4,3,2,1,0:T(8,128)S(1)} %copy-done.2, bf16[1024,512]{1,0:T(8,128)(2,1)S(1)} %copy-done), custom_call_target="tpu_custom_call" | custom-call | tf_op jit(solution)/shard_map/pallas_call | solution.py:271
  37.4 0.0 copy-start.1
  37.5 0.0 copy-start.3
  37.5 0.0 copy-start.5
  37.5 0.0 copy-start.6
  37.5 0.0 copy-start.7
  37.5 24.9 %all_to_all.31.rows_ref = f32[32,4,8,128]{3,2,1,0:T(8,128)S(1)} all-to-all(f32[32,4,8,128]{3,2,1,0:T(8,128)S(1)} %shard_map.101), channel_id=1, replica_groups={{27,26,25,24,31,30,29,28,19,18,17,16,23,22,21,20,11,10,9,8,15,14,13,12,..., dimensions={0} | all-to-all | bytes 1048576 | tf_op jit(solution)/shard_map/all_to_all | solution.py:283
  62.4 0.0 copy-done.1
  62.4 0.0 copy-done.3
  62.4 0.0 copy-done.5
  62.4 0.0 copy-done.6
  62.4 0.0 copy-done.7
  62.4 0.8 shard_map.102
  63.2 15.1 %all_to_all.32.sent_ref = f32[32,1,640]{2,1,0:T(1,128)S(1)} all-to-all(f32[32,1,640]{2,1,0:T(1,128)S(1)} %get-tuple-element.11), channel_id=1, replica_groups={{27,26,25,24,31,30,29,28,19,18,17,16,23,22,21,20,11,10,9,8,15,14,13,12,..., dimensions={0} | all-to-all | bytes 163840 | tf_op jit(solution)/shard_map/all_to_all | solution.py:283
  78.4 5.7 %shard_map.103 = f32[32,4,8,128]{3,2,1,0:T(8,128)S(1)} custom-call(s32[32,32]{1,0:T(8,128)S(1)} %copy-done.4, f32[32,1,640]{2,1,0:T(1,128)S(1)} %all_to_all.32.sent_ref, f32[1,2,32,8,256]{4,3,2,1,0:T(8,128)S(1)} %copy-done.2, bf16[1024,512]{1,0:T(8,128)(2,1)S(1)} %copy-done), custom_call_target="tpu_custom_call" | custom-call | tf_op jit(solution)/shard_map/pallas_call | solution.py:271
  84.1 25.0 %all_to_all.33.rows_ref = f32[32,4,8,128]{3,2,1,0:T(8,128)S(1)} all-to-all(f32[32,4,8,128]{3,2,1,0:T(8,128)S(1)} %shard_map.103), channel_id=1, replica_groups={{27,26,25,24,31,30,29,28,19,18,17,16,23,22,21,20,11,10,9,8,15,14,13,12,..., dimensions={0} | all-to-all | bytes 1048576 | tf_op jit(solution)/shard_map/all_to_all | solution.py:283
  109.1 0.4 shard_map.104
  109.5 9.1 %all_to_all.34 = f32[4,128,128]{2,1,0:T(8,128)S(1)} all-to-all(f32[4,128,128]{2,1,0:T(8,128)S(1)} %shard_map.104), channel_id=1, replica_groups={{64,32,0,96},{192,160,128,224},{320,288,256,352},{448,416,384,480},{257..., dimensions={0} | all-to-all | bytes 524288 | tf_op jit(solution)/shard_map/all_to_all | solution.py:297
  118.6 9.6 %all_to_all.35 = f32[4,128,128]{2,1,0:T(8,128)S(1)} all-to-all(f32[4,128,128]{2,1,0:T(8,128)S(1)} %broadcast_in_dim.10), channel_id=1, replica_groups={{256,128,0,384},{288,160,32,416},{320,192,64,448},{352,224,96,480},{65,..., dimensions={0} | all-to-all | bytes 524288 | tf_op jit(solution)/shard_map/all_to_all | solution.py:297
  128.2 0.6 fusion
  (2 shorter events, 0.0 us)
Async XLA Ops:
  0.0 32.2 %copy-start = (bf16[1024,512]{1,0:T(8,128)(2,1)S(1)}, bf16[1024,512]{1,0:T(8,128)(2,1)}, u32[]{:S(2)}) copy-start(bf16[1024,512]{1,0:T(8,128)(2,1)} %constant.7.clone.table_ref) | copy-start | bytes 3145732
  2.4 29.8 %copy-start.2 = (f32[1,2,32,8,256]{4,3,2,1,0:T(8,128)S(1)}, f32[1,2,32,8,256]{4,3,2,1,0:T(8,128)}, u32[]{:S(2)}) copy-start(f32[1,2,32,8,256]{4,3,2,1,0:T(8,128)} %green_ref.3) | copy-start | bytes 1572868
  2.4 29.8 %copy-start.4 = (s32[32,32]{1,0:T(8,128)S(1)}, s32[32,32]{1,0:T(8,128)}, u32[]{:S(2)}) copy-start(s32[32,32]{1,0:T(8,128)} %get-tuple-element.9.place_any) | copy-start | bytes 12292
  37.4 24.9 %copy-start.1 = (bf16[256,1024]{1,0:T(8,128)(2,1)S(1)}, bf16[256,1024]{1,0:T(8,128)(2,1)}, u32[]{:S(2)}) copy-start(bf16[256,1024]{1,0:T(8,128)(2,1)} %constant.8.clone.table_ref) | copy-start | bytes 1572868
  37.5 24.9 %copy-start.3 = (f32[1,2,2,1,128,128]{5,4,3,2,1,0:T(8,128)S(1)}, f32[1,2,2,1,128,128]{5,4,3,2,1,0:T(8,128)}, u32[]{:S(2)}) copy-start(f32[1,2,2,1,128,128]{5,4,3,2,1,0:T(8,128)} %field_ref.1) | copy-start | bytes 786436
  37.5 24.9 %copy-start.5 = (f32[1,2,2,1,128]{4,3,2,1,0:T(1,128)S(1)}, f32[1,2,2,1,128]{4,3,2,1,0:T(1,128)}, u32[]{:S(2)}) copy-start(f32[1,2,2,1,128]{4,3,2,1,0:T(1,128)} %seen_ref.1) | copy-start | bytes 6148
  37.5 24.9 %copy-start.6 = (f32[1,2,1,128]{3,2,1,0:T(1,128)S(1)}, f32[1,2,1,128]{3,2,1,0:T(1,128)}, u32[]{:S(2)}) copy-start(f32[1,2,1,128]{3,2,1,0:T(1,128)} %error_ref.1) | copy-start | bytes 3076
  37.5 24.9 %copy-start.7 = (s32[1,128]{1,0:T(1,128)S(1)}, s32[1,128]{1,0:T(1,128)}, u32[]{:S(2)}) copy-start(s32[1,128]{1,0:T(1,128)} %station_ref.1) | copy-start | bytes 1540

commit v9 on v8

--- a/solution.py
+++ b/solution.py
@@ -15,8 +15,9 @@
 LAYERS = 32
 ROWS = 8
 KERNELS = 32
+KERN_ROWS = 6 * ROWS
 POLS = 2
-GROUP = 4
+GROUP = 2
 STEP = 16
 RING = 4
 LEAD = 27
@@ -85,7 +86,7 @@
     ]
     cells = jnp.concatenate([stacks[0], stacks[1], stacks[0]], axis=0)
     copies[3].wait()
-    place_ref[...] = pair_ref[...] * (3 * ROWS)
+    place_ref[...] = pair_ref[...] * KERN_ROWS
     copies[2].wait()
     rows = jnp.dot(thrice(table_ref[...], 1), cells, preferred_element_type=F32)
     for c in range(2):
@@ -95,61 +96,61 @@
 
 
 def mix_rows(rows_ref, green_ref, place_ref, places, table_ref, out_ref, spec_ref, kern_ref, mixed_ref):
-    lanes = [slice(h * CELLS, (h + 1) * CELLS) for h in range(2)]
     forward = thrice(table_ref[: 2 * WAVES], 0)
     for p in range(POLS):
         flat = [rows_ref[:, 2 * p + c].reshape(LAYERS * ROWS, CELLS) for c in range(2)]
         both = jnp.concatenate(flat, axis=1)
         spec = jnp.dot(split_cat(both, 1), forward, preferred_element_type=F32)
-        h = p
-        g_re = green_ref[0, 0, :, :, lanes[h]]
-        g_im = green_ref[0, 1, :, :, lanes[h]]
-        kern_ref[h, :, 0:ROWS] = g_re + g_im
-        kern_ref[h, :, ROWS : 2 * ROWS] = g_re
-        kern_ref[h, :, 2 * ROWS :] = g_im
+        if p == 0:
+            for h in range(2):
+                g_re = green_ref[0, 0, :, :, h * CELLS : (h + 1) * CELLS]
+                g_im = green_ref[0, 1, :, :, h * CELLS : (h + 1) * CELLS]
+                for k, value in enumerate((g_re + g_im, g_re, g_im)):
+                    at = (3 * h + k) * ROWS
+                    kern_ref[:, at : at + ROWS] = value
         for h in range(2):
             re = spec[:, h * CELLS : (h + 1) * CELLS].reshape(LAYERS, ROWS, CELLS)
             im = spec[:, WAVES + h * CELLS : WAVES + (h + 1) * CELLS].reshape(LAYERS, ROWS, CELLS)
             for k, value in enumerate((re, im - re, re + im)):
-                at = (3 * p + k) * ROWS
-                spec_ref[h, :, at : at + ROWS] = value
+                at = ((h * POLS + p) * 3 + k) * ROWS
+                spec_ref[:, at : at + ROWS] = value
 
     places.wait()
-    kern = [kern_ref.at[h].reshape(KERNELS * 3 * ROWS, CELLS) for h in range(2)]
-    for h in range(2):
-
-        def one_group(group, carry, h=h):
-            first = group * GROUP
-            first_layer = (group ^ (LEAD // GROUP)) * GROUP
-
-            def some_sources(chunk, sums):
-                sums = list(sums)
-                for s in range(STEP):
-                    j = chunk * STEP + s
-                    src = [spec_ref[h, j, k * ROWS : (k + 1) * ROWS] for k in range(3 * POLS)]
-                    layer = (chunk ^ (LEAD // STEP)) * STEP + (s ^ (LEAD % STEP))
-                    for r in range(GROUP):
-                        place = place_ref[first_layer + (r ^ (LEAD % GROUP)), layer]
+    kern = kern_ref.reshape(KERNELS * KERN_ROWS, CELLS)
+    terms = [(r, h, p, k) for r in range(GROUP) for h in range(2) for k in range(3) for p in range(POLS)]
+
+    def one_group(group, carry):
+        first = group * GROUP
+        first_layer = (group ^ (LEAD // GROUP)) * GROUP
+
+        def some_sources(chunk, sums):
+            sums = dict(zip(terms, sums))
+            for s in range(STEP):
+                j = chunk * STEP + s
+                src = [spec_ref[j, k * ROWS : (k + 1) * ROWS] for k in range(6 * POLS)]
+                layer = (chunk ^ (LEAD // STEP)) * STEP + (s ^ (LEAD % STEP))
+                for r in range(GROUP):
+                    place = place_ref[first_layer + (r ^ (LEAD % GROUP)), layer]
+                    for h in range(2):
                         for k in range(3):
-                            row = pl.multiple_of(place + k * ROWS, ROWS)
-                            factor = kern[h][pl.ds(row, ROWS), :]
+                            row = pl.multiple_of(place + (3 * h + k) * ROWS, ROWS)
+                            factor = kern[pl.ds(row, ROWS), :]
                             for p in range(POLS):
-                                at = (r * POLS + p) * 3 + k
-                                sums[at] = sums[at] + factor * src[3 * p + k]
-                return tuple(sums)
-
-            zero = jnp.zeros((ROWS, CELLS), F32)
-            sums = lax.fori_loop(
-                0, LAYERS // STEP, some_sources, (zero,) * (GROUP * POLS * 3)
-            )
-            for r in range(GROUP):
+                                sums[r, h, p, k] = sums[r, h, p, k] + factor * src[(h * POLS + p) * 3 + k]
+            return tuple(sums[term] for term in terms)
+
+        zero = jnp.zeros((ROWS, CELLS), F32)
+        sums = lax.fori_loop(0, LAYERS // STEP, some_sources, (zero,) * len(terms))
+        sums = dict(zip(terms, sums))
+        for r in range(GROUP):
+            for h in range(2):
                 for p in range(POLS):
-                    one, two, three = sums[(r * POLS + p) * 3 : (r * POLS + p) * 3 + 3]
+                    one, two, three = (sums[r, h, p, k] for k in range(3))
                     mixed_ref[p, first + r, :, h * CELLS : (h + 1) * CELLS] = one - three
                     mixed_ref[p, first + r, :, WAVES + h * CELLS : WAVES + (h + 1) * CELLS] = one + two
-            return carry
-
-        lax.fori_loop(0, LAYERS // GROUP, one_group, 0)
+        return carry
+
+    lax.fori_loop(0, LAYERS // GROUP, one_group, 0)
 
     high, low = table_ref[2 * WAVES :, :WAVES], table_ref[2 * WAVES :, WAVES:]
     inverse = jnp.concatenate([high, high, low], axis=0)
@@ -306,8 +307,8 @@
     x_fwd, y_both, x_inv = dft_blocks()
     rows_shape = jax.ShapeDtypeStruct((LAYERS, 4, ROWS, CELLS), F32)
     scratch = (
-        pltpu.VMEM((2, LAYERS, 3 * POLS * ROWS, CELLS), F32),
-        pltpu.VMEM((2, KERNELS, 3 * ROWS, CELLS), F32),
+        pltpu.VMEM((LAYERS, 6 * POLS * ROWS, CELLS), F32),
+        pltpu.VMEM((KERNELS, KERN_ROWS, CELLS), F32),
         pltpu.VMEM((POLS, LAYERS, ROWS, 2 * WAVES), F32),
         pltpu.SMEM(pair_table.shape, jnp.int32),
         pltpu.SemaphoreType.DMA(()),

time: 129 us -> 130 us (level)
  no operation moved by 1% of the time
where the time goes in v9:
time: 130 us; the launch traced here: 129 us
  blocking collectives  113 us (87%)
  Pallas kernels  14.9 us (11%)
    all_to_all x4, blocking collectives, over_layers(): lax.all_to_all(values, 'layer', split_axis=0, concat_axis=0, tiled=True,...  94.8 us
    all_to_all x2, blocking collectives, sum_over_freq(): lax.all_to_all(copies, ('freq', 'layer'), split_axis=0, concat_axis=0, ti...  18.7 us
    pallas_call x4, Pallas kernels, call(): pl.pallas_call(kernel, out_shape=out_shape, in_specs=specs, out_specs=out...  12.5 us

profile of v9, /device:TPU:60, one launch (start us, length us, event | category | flops | bytes accessed | tf_op | source)
XLA Modules:
  0.0 129.2 jit_solution(17973262813603904432)
XLA Ops:
  0.0 0.0 copy-start
  0.0 2.4 %shard_map.100 = (f32[32,4,8,128]{3,2,1,0:T(8,128)}, s32[32,32]{1,0:T(8,128)}) custom-call(f32[1,128,128]{2,1,0:T(8,128)} %cond_hbm.1, f32[1,2,2,1,128,128]{5,4,3,2,1,0:T(8,128)} %field_ref.1, bf16[256,512]{1,0:T(8,128)(2,1)} %constant.6.clone.table_hbm, s32[32,32]{1,0:T(8,128)} %pair_hbm.1), custom_call_target="tpu_custom_call" | custom-call | tf_op jit(solution)/shard_map/pallas_call | solution.py:316
  2.4 0.0 copy-start.2
  2.4 0.0 copy-start.4
  2.4 29.8 %all_to_all.30.rows_ref = f32[32,4,8,128]{3,2,1,0:T(8,128)S(1)} all-to-all(f32[32,4,8,128]{3,2,1,0:T(8,128)} %get-tuple-element.10), channel_id=1, replica_groups={{27,26,25,24,31,30,29,28,19,18,17,16,23,22,21,20,11,10,9,8,15,14,13,12,..., dimensions={0} | all-to-all | bytes 1048576 | tf_op jit(solution)/shard_map/all_to_all | solution.py:284
  32.2 0.0 copy-done
  32.2 0.0 copy-done.2
  32.2 0.0 copy-done.4
  32.2 5.4 %shard_map.101 = f32[32,4,8,128]{3,2,1,0:T(8,128)S(1)} custom-call(s32[32,32]{1,0:T(8,128)S(1)} %copy-done.4, f32[32,4,8,128]{3,2,1,0:T(8,128)S(1)} %all_to_all.30.rows_ref, f32[1,2,32,8,256]{4,3,2,1,0:T(8,128)S(1)} %copy-done.2, bf16[1024,512]{1,0:T(8,128)(2,1)S(1)} %copy-done), custom_call_target="tpu_custom_call" | custom-call | tf_op jit(solution)/shard_map/pallas_call | solution.py:272
  37.6 0.0 copy-start.1
  37.6 0.0 copy-start.3
  37.6 0.0 copy-start.5
  37.7 0.0 copy-start.6
  37.7 0.0 copy-start.7
  37.7 24.9 %all_to_all.31.rows_ref = f32[32,4,8,128]{3,2,1,0:T(8,128)S(1)} all-to-all(f32[32,4,8,128]{3,2,1,0:T(8,128)S(1)} %shard_map.101), channel_id=1, replica_groups={{27,26,25,24,31,30,29,28,19,18,17,16,23,22,21,20,11,10,9,8,15,14,13,12,..., dimensions={0} | all-to-all | bytes 1048576 | tf_op jit(solution)/shard_map/all_to_all | solution.py:284
  62.6 0.0 copy-done.1
  62.6 0.0 copy-done.3
  62.6 0.0 copy-done.5
  62.6 0.0 copy-done.6
  62.6 0.0 copy-done.7
  62.6 0.8 shard_map.102
  63.4 15.1 %all_to_all.32.sent_ref = f32[32,1,640]{2,1,0:T(1,128)S(1)} all-to-all(f32[32,1,640]{2,1,0:T(1,128)S(1)} %get-tuple-element.11), channel_id=1, replica_groups={{27,26,25,24,31,30,29,28,19,18,17,16,23,22,21,20,11,10,9,8,15,14,13,12,..., dimensions={0} | all-to-all | bytes 163840 | tf_op jit(solution)/shard_map/all_to_all | solution.py:284
  78.6 5.9 %shard_map.103 = f32[32,4,8,128]{3,2,1,0:T(8,128)S(1)} custom-call(s32[32,32]{1,0:T(8,128)S(1)} %copy-done.4, f32[32,1,640]{2,1,0:T(1,128)S(1)} %all_to_all.32.sent_ref, f32[1,2,32,8,256]{4,3,2,1,0:T(8,128)S(1)} %copy-done.2, bf16[1024,512]{1,0:T(8,128)(2,1)S(1)} %copy-done), custom_call_target="tpu_custom_call" | custom-call | tf_op jit(solution)/shard_map/pallas_call | solution.py:272
  84.5 25.0 %all_to_all.33.rows_ref = f32[32,4,8,128]{3,2,1,0:T(8,128)S(1)} all-to-all(f32[32,4,8,128]{3,2,1,0:T(8,128)S(1)} %shard_map.103), channel_id=1, replica_groups={{27,26,25,24,31,30,29,28,19,18,17,16,23,22,21,20,11,10,9,8,15,14,13,12,..., dimensions={0} | all-to-all | bytes 1048576 | tf_op jit(solution)/shard_map/all_to_all | solution.py:284
  109.5 0.4 shard_map.104
  109.9 9.1 %all_to_all.34 = f32[4,128,128]{2,1,0:T(8,128)S(1)} all-to-all(f32[4,128,128]{2,1,0:T(8,128)S(1)} %shard_map.104), channel_id=1, replica_groups={{64,32,0,96},{192,160,128,224},{320,288,256,352},{448,416,384,480},{257..., dimensions={0} | all-to-all | bytes 524288 | tf_op jit(solution)/shard_map/all_to_all | solution.py:298
  119.0 9.6 %all_to_all.35 = f32[4,128,128]{2,1,0:T(8,128)S(1)} all-to-all(f32[4,128,128]{2,1,0:T(8,128)S(1)} %broadcast_in_dim.10), channel_id=1, replica_groups={{256,128,0,384},{288,160,32,416},{320,192,64,448},{352,224,96,480},{65,..., dimensions={0} | all-to-all | bytes 524288 | tf_op jit(solution)/shard_map/all_to_all | solution.py:298
  128.6 0.6 fusion
  (2 shorter events, 0.0 us)
Async XLA Ops:
  0.0 32.2 %copy-start = (bf16[1024,512]{1,0:T(8,128)(2,1)S(1)}, bf16[1024,512]{1,0:T(8,128)(2,1)}, u32[]{:S(2)}) copy-start(bf16[1024,512]{1,0:T(8,128)(2,1)} %constant.7.clone.table_ref) | copy-start | bytes 3145732
  2.4 29.8 %copy-start.2 = (f32[1,2,32,8,256]{4,3,2,1,0:T(8,128)S(1)}, f32[1,2,32,8,256]{4,3,2,1,0:T(8,128)}, u32[]{:S(2)}) copy-start(f32[1,2,32,8,256]{4,3,2,1,0:T(8,128)} %green_ref.3) | copy-start | bytes 1572868
  2.4 29.8 %copy-start.4 = (s32[32,32]{1,0:T(8,128)S(1)}, s32[32,32]{1,0:T(8,128)}, u32[]{:S(2)}) copy-start(s32[32,32]{1,0:T(8,128)} %get-tuple-element.9.place_any) | copy-start | bytes 12292
  37.6 24.9 %copy-start.1 = (bf16[256,1024]{1,0:T(8,128)(2,1)S(1)}, bf16[256,1024]{1,0:T(8,128)(2,1)}, u32[]{:S(2)}) copy-start(bf16[256,1024]{1,0:T(8,128)(2,1)} %constant.8.clone.table_ref) | copy-start | bytes 1572868
  37.6 24.9 %copy-start.3 = (f32[1,2,2,1,128,128]{5,4,3,2,1,0:T(8,128)S(1)}, f32[1,2,2,1,128,128]{5,4,3,2,1,0:T(8,128)}, u32[]{:S(2)}) copy-start(f32[1,2,2,1,128,128]{5,4,3,2,1,0:T(8,128)} %field_ref.1) | copy-start | bytes 786436
  37.6 24.9 %copy-start.5 = (f32[1,2,2,1,128]{4,3,2,1,0:T(1,128)S(1)}, f32[1,2,2,1,128]{4,3,2,1,0:T(1,128)}, u32[]{:S(2)}) copy-start(f32[1,2,2,1,128]{4,3,2,1,0:T(1,128)} %seen_ref.1) | copy-start | bytes 6148
  37.7 24.9 %copy-start.6 = (f32[1,2,1,128]{3,2,1,0:T(1,128)S(1)}, f32[1,2,1,128]{3,2,1,0:T(1,128)}, u32[]{:S(2)}) copy-start(f32[1,2,1,128]{3,2,1,0:T(1,128)} %error_ref.1) | copy-start | bytes 3076
  37.7 24.9 %copy-start.7 = (s32[1,128]{1,0:T(1,128)S(1)}, s32[1,128]{1,0:T(1,128)}, u32[]{:S(2)}) copy-start(s32[1,128]{1,0:T(1,128)} %station_ref.1) | copy-start | bytes 1540
